TPU v7x, 32 devices: a whole 2x2x4 slice. The times are simulated.
32 devices in a mesh: groups: 2 (over y), inst: 4 (over z), mp: 4 (over x, core).
Axes of the slice: x: 2, y: 2, z: 4, core: 2. Of those that a mesh axis runs over, the one named last changes fastest.
Arguments:
- hidden_states: bfloat16 [3, 64, 5120], P(None, ('groups', 'inst'), 'mp'), parts along dimension 1, may hold values from -6 to 6
- kv_weight: bfloat16 [5120, 1024], P('mp'), may hold values from -0.078125 to 0.078125
- key_gain: float32 [128], replicated, may hold values from 0.1 to 1.9
- queries: bfloat16 [3, 64, 4096], P(None, ('groups', 'inst')), parts along dimension 1, may hold values from -128 to 128
- kv_pool: bfloat16 [8, 40, 16, 1024], P(('groups', 'inst'), 'mp'), parts along dimension 0, may hold values from -6 to 6
- page_table: int32 [64, 1, 4], P(('groups', 'inst'), None, 'mp'), parts along dimension 0, may hold values from 0 to 9, as said below
- lengths: int32 [64], P(('groups', 'inst')), parts along dimension 0, may hold values from 1 to 61, 976 in all
- mig_dest: int32 [8, 2], P('groups'), parts along dimension 0, may hold values from 0 to 3, as said below
- mig_local: int32 [8, 2], P('groups'), parts along dimension 0, may hold values from 0 to 7, as said below
- mig_slots: int32 [8, 2, 1, 4], P(('groups', 'inst'), None, None, 'mp'), parts along dimension 0, may hold values from 0 to 9, as said below
Outputs:
- attended: bfloat16 [3, 64, 4096], P(None, ('groups', 'inst'), 'mp'), parts along dimension 1
There are 2 independent parts, one for each index of `groups`. A program takes and returns all parts, laid end to end along the dimension named above; an argument that names none is the same for every part. Nothing has to cross between parts.
Inputs may be any that keep to these rules, and one draw needn't show every extreme that they name: For every instance and m, the slots page_table[r, j, m] of the instance's 8 requests and mig_slots[i, u, j, m] together name every slot of block m exactly once. `mig_slots`: see page_table. mig_dest[i, u] differs from i; every instance receives exactly 2 requests; in every draw some instance sends exactly 1 request to one other and none sends more. The pairs (mig_dest, mig_local) name distinct requests.
All inputs are finite; a program needn't handle non-finite values. No bound on the sum of `lengths` on one device may be relied on, other than what follows from the above.
Results may differ from a plain program's by a relative error of at most 0.0035.
Values may be sent and summed in bfloat16 or wider, within the bound.
A program may use at most 64 MiB of HBM per device.

v0:
```python
import math

import jax
import jax.numpy as jnp
from jax import lax
from jax.sharding import PartitionSpec as P


def rotary(keys, positions):
    half = keys.shape[-1] // 2
    freq = jnp.exp(
        -(2.0 * jnp.arange(half).astype(jnp.float32) / keys.shape[-1]) * math.log(1000000.0)
    )
    angle = positions.astype(jnp.float32)[..., None] * freq
    cosine = jnp.cos(angle)
    sine = jnp.sin(angle)
    first = keys[..., :half]
    second = keys[..., half:]
    return jnp.concatenate(
        [first * cosine - second * sine, second * cosine + first * sine], axis=-1
    )


def new_entries(projected, key_gain, positions):
    keys = projected[..., 0, :]
    values = projected[..., 1, :]
    factor = lax.rsqrt(jnp.mean(keys * keys, axis=-1, keepdims=True) + 1e-06)
    keys = rotary(keys * factor * key_gain, positions[:, :, None])
    return jnp.stack([keys, values], axis=-2).reshape(positions.shape + (-1,)).astype(jnp.bfloat16)


def local(
    hidden_states,
    kv_weight,
    key_gain,
    queries,
    kv_pool,
    page_table,
    lengths,
    mig_dest,
    mig_local,
    mig_slots,
):
    steps = hidden_states.shape[0]
    requests = hidden_states.shape[1]
    head_dim = key_gain.shape[0]
    width = kv_weight.shape[1]
    kv_heads = width // (2 * head_dim)
    heads = queries.shape[2] // head_dim
    group = heads // kv_heads
    partial_sum = jnp.einsum(
        "trd,dc->trc", hidden_states, kv_weight, preferred_element_type=jnp.float32
    )
    projected = lax.psum(partial_sum, "mp").reshape(steps, requests, kv_heads, 2, head_dim)
    positions = lengths[None, :] + jnp.arange(steps, dtype=jnp.int32)[:, None]
    fresh = new_entries(projected, key_gain, positions)
    inst_index = lax.axis_index("inst")
    model_count = lax.axis_size("mp")
    model_index = lax.axis_index("mp")
    pool = kv_pool[0]
    pool_dev = pool.shape[0]
    page_len = pool.shape[1]
    depth = page_table.shape[1]
    migrants = mig_dest.shape[1]
    table = page_table[:, :, 0]
    leaving = pool[mig_slots[0, :, :, 0]].reshape(migrants, depth * page_len * width)
    store = pool.reshape(pool_dev, page_len * width)
    target_flat = mig_dest.reshape(-1)
    local_flat = mig_local.reshape(-1)
    slot_rows = jnp.where((target_flat == inst_index)[:, None], table[local_flat], pool_dev)
    store = store.at[slot_rows.reshape(-1)].set(
        lax.all_gather(leaving, "inst", axis=0, tiled=True), mode="drop"
    )
    page_number = positions // page_len
    holder = page_number % model_count
    deeper = page_number // model_count
    offset = positions % page_len
    slot_index = table[jnp.arange(requests)[None, :], deeper]
    flat_index = jnp.where(
        holder == model_index, slot_index * page_len + offset, pool_dev * page_len
    )
    cached = (
        store.reshape(pool_dev * page_len, width)
        .at[flat_index.reshape(-1)]
        .set(fresh.reshape(steps * requests, width), mode="drop")
        .reshape(pool_dev, page_len, width)
    )
    held = cached[table].reshape(requests, depth * page_len, kv_heads, 2, head_dim)
    token_place = (
        (jnp.arange(depth)[:, None] * model_count + model_index) * page_len
        + jnp.arange(page_len)[None, :]
    ).reshape(-1)
    query = queries.reshape(steps, requests, kv_heads, group, head_dim)
    scores = jnp.einsum(
        "trhgd,rkhd->trhgk", query, held[..., 0, :], preferred_element_type=jnp.float32
    ) / math.sqrt(head_dim)
    valid = (token_place[None, None, :] <= positions[:, :, None])[:, :, None, None, :]
    scores = jnp.where(valid, scores, -1e30)
    peak = jnp.max(scores, axis=-1)
    weights = jnp.where(valid, jnp.exp(scores - peak[..., None]), 0.0)
    total = jnp.sum(weights, axis=-1)
    summed = jnp.einsum(
        "trhgk,rkhd->trhgd",
        weights,
        held[..., 1, :].astype(jnp.float32),
        precision=lax.Precision.HIGHEST,
    )
    peak = peak.reshape(steps, requests, heads)
    total = total.reshape(steps, requests, heads)
    summed = summed.reshape(steps, requests, heads, head_dim)
    portion = heads // model_count
    peak = peak.reshape(steps, requests, model_count, portion)
    total = total.reshape(steps, requests, model_count, portion)
    summed = summed.reshape(steps, requests, model_count, portion, head_dim)
    peak, total, summed = (
        lax.all_to_all(peak, "mp", split_axis=2, concat_axis=2, tiled=True),
        lax.all_to_all(total, "mp", split_axis=2, concat_axis=2, tiled=True),
        lax.all_to_all(summed, "mp", split_axis=2, concat_axis=2, tiled=True),
    )
    highest = jnp.max(peak, axis=2)
    factor = jnp.exp(peak - highest[:, :, None, :])
    total = jnp.sum(total * factor, axis=2)
    summed = jnp.sum(summed * factor[..., None], axis=2)
    result = (summed / total[..., None]).reshape(steps, requests, portion * head_dim)
    return result.astype(jnp.bfloat16)


def solution(mesh):
    placed = (
        P(None, ("groups", "inst"), "mp"),
        P("mp", None),
        P(),
        P(None, ("groups", "inst"), None),
        P(("groups", "inst"), "mp", None, None),
        P(("groups", "inst"), None, "mp"),
        P(("groups", "inst")),
        P("groups", None),
        P("groups", None),
        P(("groups", "inst"), None, None, "mp"),
    )
    return jax.shard_map(
        local,
        mesh=mesh,
        in_specs=placed,
        out_specs=P(None, ("groups", "inst"), "mp"),
        check_vma=False,
    )
```

profile of v0, /device:TPU:0, one launch (start us, length us, event | category | flops | bytes accessed | tf_op | source)
XLA Modules:
  0.0 84.1 jit_solution(1793530371518237266)
XLA Ops:
  6.5 0.0 copy-start
  6.5 0.0 copy-start.2
  6.6 0.0 copy-start.1
  6.6 0.0 all-reduce.2.cloned.1.call-start
  6.6 1.7 %copy-done = bf16[1280,1024]{1,0:T(8,128)(2,1)S(1)} copy-done((bf16[1280,1024]{1,0:T(8,128)(2,1)S(1)}, bf16[1280,1024]{1,0:T(8,128)(2,1)}, u32[]{:S(2)}) %copy-start) | copy-done | bytes 2621464
  8.3 1.9 %fusion = f32[3,8,1024]{2,1,0:T(8,128)} fusion(bf16[3,8,1280]{2,1,0:T(8,128)(2,1)} %param.10, bf16[1280,1024]{1,0:T(8,128)(2,1)S(1)} %copy-done), kind=kOutput, calls=%fused_computation.6 | convolution fusion | flops 62914560 | bytes 2781184 | tf_op jit(solution)/shard_map/trd,dc->trc/dot_general | solution.py:51
  10.2 0.0 all-reduce.2.cloned.1.call-update
  10.2 0.0 copy-done.4
  10.3 0.1 add.202
  10.4 0.1 copy.53
  10.5 0.0 copy-done.6
  10.5 0.1 copy.49
  10.6 0.1 eq.37
  10.7 0.0 copy-done.5
  10.7 0.1 copy.50
  10.8 0.1 reshape.497
  10.9 0.0 copy-done.7
  10.9 0.0 copy-done.2
  10.9 0.6 gather_fusion.1
  11.5 0.1 reshape.522
  11.6 0.0 copy-done.1
  11.6 0.6 pad_clamp_fusion
  12.2 0.6 gather_fusion
  12.8 0.7 gather_fusion.2
  13.6 0.6 fusion.22
  14.2 0.7 multiply_cosine_fusion
  14.9 0.1 broadcast_compare_fusion
  15.0 16.3 %all-gather = bf16[4,2,16384]{2,1,0:T(2,128)(2,1)} all-gather(bf16[1,2,16384]{2,1,0:T(2,128)(2,1)S(1)} %reshape.558), channel_id=1, replica_groups=mesh['groups'=2,'inst'=4,'mp'=4] {'inst'}, dimensions={0}, use_global_device_ids=true | all-gather | bytes 327680 | tf_op jit(solution)/shard_map/all_gather | solution.py:72
  31.4 0.3 copy.70
  31.7 1.1 %reshape.559 = bf16[8,16384]{1,0:T(8,128)(2,1)S(1)} reshape(bf16[4,2,16384]{2,1,0:T(2,128)(2,1)} %all-gather) | data formatting | bytes 524288
  32.7 1.3 %scatter_fusion = bf16[10,16384]{1,0:T(8,128)(2,1)S(1)} fusion(bf16[10,16384]{1,0:T(8,128)(2,1)S(1)} %bitcast.82, s32[8]{0:T(128)S(1)} %fusion.20, bf16[8,16384]{1,0:T(8,128)(2,1)S(1)} %reshape.559), kind=kCustom, calls=%fused_computation.4 | custom fusion | bytes 786464 | tf_op jit(solution)/shard_map/scatter | solution.py:71
  34.0 0.2 reshape.499
  34.2 0.0 copy-start.3
  34.2 10.2 %all-reduce.2.cloned.1.call-done = f32[3,8,4,2,128]{4,1,3,2,0:T(8,128)} async-done(((f32[3,8,4,2,128]{4,1,3,2,0:T(8,128)}), f32[3,8,4,2,128]{4,1,3,2,0:T(8,128)}) %all-reduce.2.cloned.1.call-update) | async-done | bytes 98320 | tf_op jit(solution)/shard_map/psum | solution.py:54
  44.4 0.9 %multiply_reduce_fusion.2 = f32[3,8,4]{1,2,0:T(4,128)S(1)} fusion(f32[3,8,4,2,128]{4,1,3,2,0:T(8,128)} %all-reduce.2.cloned.1.call-done), kind=kLoop, calls=%fused_computation.30 | loop fusion | flops 24480 | bytes 49536 | tf_op jit(solution)/shard_map/reduce_sum | solution.py:27
  45.3 0.9 %multiply_multiply_fusion = f32[3,8,4,128]{3,1,2,0:T(8,128)S(1)} fusion(f32[3,8,4,2,128]{4,1,3,2,0:T(8,128)} %all-reduce.2.cloned.1.call-done, f32[128]{0:T(128)} %param.12, f32[3,8,4]{1,2,0:T(4,128)S(1)} %add_rsqrt_fusion), kind=kLoop, calls=%fused_computation.29 | loop fusion | flops 24576 | bytes 99200 | tf_op jit(solution)/shard_map/mul | solution.py:28
  46.2 0.8 subtract_convert_fusion
  47.0 0.1 maximum_bitcast_fusion
  47.1 0.8 slice.49
  47.9 1.0 %scatter_fusion.1 = bf16[160,1024]{1,0:T(8,128)(2,1)S(1)} fusion(bf16[160,1024]{1,0:T(8,128)(2,1)S(1)} %reshape.499, s32[24]{0:T(128)} %fusion.22, bf16[24,1024]{1,0:T(8,128)(2,1)S(1)} %bitcast.88), kind=kCustom, calls=%fused_computation.5 | custom fusion | bytes 147552 | tf_op jit(solution)/shard_map/scatter | solution.py:85
  49.0 0.7 gather_fusion.3
  49.7 0.2 reshape.502
  49.8 0.5 fusion.26
  50.3 0.0 copy-done.3
  50.3 0.4 fusion.27
  50.7 0.7 reshape.564
  51.4 3.2 %all-to-all-start.1 = ((f32[4,1,192]{2,1,0:T(1,128)}), f32[4,1,192]{2,1,0:T(1,128)S(1)}, u32[]{:S(2)}, u32[]{:S(2)}) async-start(f32[4,1,192]{2,1,0:T(1,128)} %reshape.564), calls=%async_computation.1 | async-start | bytes 8192 | tf_op jit(solution)/shard_map/all_to_all | solution.py:116
  54.6 0.4 fusion.4
  55.0 0.7 reshape.566
  55.7 2.7 %all-to-all-done.1 = f32[4,1,192]{2,1,0:T(1,128)S(1)} async-done(((f32[4,1,192]{2,1,0:T(1,128)}), f32[4,1,192]{2,1,0:T(1,128)S(1)}, u32[]{:S(2)}, u32[]{:S(2)}) %all-to-all-start.1) | async-done | bytes 3104 | tf_op jit(solution)/shard_map/all_to_all | solution.py:116
  58.4 3.2 %all-to-all-start.2 = ((f32[4,1,192]{2,1,0:T(1,128)}), f32[4,1,192]{2,1,0:T(1,128)S(1)}, u32[]{:S(2)}, u32[]{:S(2)}) async-start(f32[4,1,192]{2,1,0:T(1,128)} %reshape.566), calls=%async_computation.2 | async-start | bytes 8192 | tf_op jit(solution)/shard_map/all_to_all | solution.py:117
  61.6 0.5 convolution_bitcast_fusion
  62.2 0.8 copy.56
  63.0 0.5 broadcast.539
  63.5 0.7 reduce
  64.1 0.1 reshape.565
  64.2 1.2 %all-to-all-done.2 = f32[4,1,192]{2,1,0:T(1,128)S(1)} async-done(((f32[4,1,192]{2,1,0:T(1,128)}), f32[4,1,192]{2,1,0:T(1,128)S(1)}, u32[]{:S(2)}, u32[]{:S(2)}) %all-to-all-start.2) | async-done | bytes 3104 | tf_op jit(solution)/shard_map/all_to_all | solution.py:117
  65.4 3.5 %all-to-all-start = ((f32[3,8,4,8,128]{4,3,0,1,2:T(8,128)}), f32[3,8,4,8,128]{4,3,0,1,2:T(8,128)S(1)}, u32[]{:S(2)}, u32[]{:S(2)}) async-start(f32[3,8,4,8,128]{4,3,0,1,2:T(8,128)} %copy.56), calls=%async_computation | async-start | bytes 786432 | tf_op jit(solution)/shard_map/all_to_all | solution.py:118
  68.9 0.7 reduce.1
  69.5 0.1 reshape.567
  69.7 6.6 %all-to-all-done = f32[3,8,4,8,128]{4,3,0,1,2:T(8,128)S(1)} async-done(((f32[3,8,4,8,128]{4,3,0,1,2:T(8,128)}), f32[3,8,4,8,128]{4,3,0,1,2:T(8,128)S(1)}, u32[]{:S(2)}, u32[]{:S(2)}) %all-to-all-start) | async-done | bytes 393248 | tf_op jit(solution)/shard_map/all_to_all | solution.py:118
  76.3 0.2 multiply_reduce_fusion
  76.4 0.1 divide_convert_fusion
  76.6 0.6 convert_element_type.32
  (26 shorter events, 0.3 us)
Async XLA Ops:
  6.5 1.7 %copy-start = (bf16[1280,1024]{1,0:T(8,128)(2,1)S(1)}, bf16[1280,1024]{1,0:T(8,128)(2,1)}, u32[]{:S(2)}) copy-start(bf16[1280,1024]{1,0:T(8,128)(2,1)} %param.11) | copy-start | bytes 7864324
  6.5 3.7 %copy-start.4 = (s32[8]{0:T(128)S(1)}, s32[8]{0:T(128)}, u32[]{:S(2)}) copy-start(s32[8]{0:T(128)} %param.16) | copy-start | bytes 100
  6.5 3.9 %copy-start.6 = (s32[4,2]{0,1:T(2,128)S(1)}, s32[4,2]{0,1:T(2,128)}, u32[]{:S(2)}) copy-start(s32[4,2]{0,1:T(2,128)} %param.17) | copy-start | bytes 100
  6.5 4.1 %copy-start.5 = (s32[4,2]{0,1:T(2,128)S(1)}, s32[4,2]{0,1:T(2,128)}, u32[]{:S(2)}) copy-start(s32[4,2]{0,1:T(2,128)} %param.18) | copy-start | bytes 100
  6.5 4.3 %copy-start.7 = (s32[1,2,1,1]{1,3,2,0:T(1,128)S(1)}, s32[1,2,1,1]{1,3,2,0:T(1,128)}, u32[]{:S(2)}) copy-start(s32[1,2,1,1]{1,3,2,0:T(1,128)} %param.19) | copy-start | bytes 28
  6.5 4.4 %copy-start.2 = (bf16[1,10,16,1024]{3,2,1,0:T(8,128)(2,1)S(1)}, bf16[1,10,16,1024]{3,2,1,0:T(8,128)(2,1)}, u32[]{:S(2)}) copy-start(bf16[1,10,16,1024]{3,2,1,0:T(8,128)(2,1)} %param.14) | copy-start | bytes 983044
  6.6 5.0 %copy-start.1 = (s32[8,1,1]{0,2,1:T(1,128)S(1)}, s32[8,1,1]{0,2,1:T(1,128)}, u32[]{:S(2)}) copy-start(s32[8,1,1]{0,2,1:T(1,128)} %param.15) | copy-start | bytes 100
  6.6 37.9 %all-reduce.2.cloned.1.call-start = ((), (), s32[]{:S(2)}) async-start(), calls=%async_computation.3 | async-start | bytes 196608 | tf_op jit(solution)/shard_map/psum | solution.py:54
  34.2 16.1 %copy-start.3 = (bf16[3,8,4096]{2,1,0:T(8,128)(2,1)S(1)}, bf16[3,8,4096]{2,1,0:T(8,128)(2,1)}, u32[]{:S(2)}) copy-start(bf16[3,8,4096]{2,1,0:T(8,128)(2,1)} %param.13) | copy-start | bytes 589828
  51.4 7.0 %all-to-all-start.1 = ((f32[4,1,192]{2,1,0:T(1,128)}), f32[4,1,192]{2,1,0:T(1,128)S(1)}, u32[]{:S(2)}, u32[]{:S(2)}) async-start(f32[4,1,192]{2,1,0:T(1,128)} %reshape.564), calls=%async_computation.1 | async-start | bytes 8192 | tf_op jit(solution)/shard_map/all_to_all | solution.py:116
  58.4 7.0 %all-to-all-start.2 = ((f32[4,1,192]{2,1,0:T(1,128)}), f32[4,1,192]{2,1,0:T(1,128)S(1)}, u32[]{:S(2)}, u32[]{:S(2)}) async-start(f32[4,1,192]{2,1,0:T(1,128)} %reshape.566), calls=%async_computation.2 | async-start | bytes 8192 | tf_op jit(solution)/shard_map/all_to_all | solution.py:117
  65.4 10.9 %all-to-all-start = ((f32[3,8,4,8,128]{4,3,0,1,2:T(8,128)}), f32[3,8,4,8,128]{4,3,0,1,2:T(8,128)S(1)}, u32[]{:S(2)}, u32[]{:S(2)}) async-start(f32[3,8,4,8,128]{4,3,0,1,2:T(8,128)} %copy.56), calls=%async_computation | async-start | bytes 786432 | tf_op jit(solution)/shard_map/all_to_all | solution.py:118
Sparse Core Ops, SparseCore 0:
  10.3 34.0 all-reduce.1
where the time goes:
time: 84.7 us; the launch traced here: 84.1 us
  waiting for transfers between devices  20.6 us (24%)
  blocking collectives  16.3 us (19%)
  local copies, waits for them, and re-layouts  13.9 us (16%)
  between operations  13.7 us (16%)
  starting transfers between devices  9.98 us (12%)
  other arithmetic  6.75 us (8%)
  matrix products  2.82 us (3%)
    all_gather x1, blocking collectives, local(): lax.all_gather(leaving, 'inst', axis=0, tiled=True)  16.3 us
    psum x1, waiting for transfers between devices, local(): lax.psum(partial_sum, 'mp').reshape(steps, requests, kv_heads, 2, head_dim)  10.2 us
    all_to_all x1, waiting for transfers between devices, local(): lax.all_to_all(summed, 'mp', split_axis=2, concat_axis=2, tiled=True)  6.56 us
    unnamed x26, local copies, waits for them, and re-layouts  4.75 us
    all_to_all x1, starting transfers between devices, local(): lax.all_to_all(summed, 'mp', split_axis=2, concat_axis=2, tiled=True)  3.46 us
    all_to_all x1, starting transfers between devices, local(): lax.all_to_all(peak, 'mp', split_axis=2, concat_axis=2, tiled=True)  3.25 us
    all_to_all x1, starting transfers between devices, local(): lax.all_to_all(total, 'mp', split_axis=2, concat_axis=2, tiled=True)  3.23 us
    all_to_all x1, waiting for transfers between devices, local(): lax.all_to_all(peak, 'mp', split_axis=2, concat_axis=2, tiled=True)  2.67 us
  transfers between devices with their start and end apart: 4, of which 4 were waited for; matrix products, arithmetic and copies ran while one was open for 14% of the time, Pallas kernels for 0%

commit v1 on v0

v1 whole, which is shorter than its diff:
```python
import functools
import math

import jax
import jax.numpy as jnp
from jax import lax
from jax.experimental import pallas as pl
from jax.experimental.pallas import tpu as pltpu
from jax.sharding import PartitionSpec as P

MESH = pl.DeviceIdType.MESH
F32 = jnp.float32
BF16 = jnp.bfloat16


def loop(count, step):
    if count <= 4:
        for index in range(count):
            step(index)
    else:
        lax.fori_loop(0, count, lambda index, carry: (step(index), carry)[1], 0)


def dot(left, right, contract=((1,), (0,))):
    return lax.dot_general(left, right, (contract, ((), ())), preferred_element_type=F32)


def weighted(weights, values):
    high = weights.astype(BF16)
    low = (weights - high.astype(F32)).astype(BF16)
    return dot(high, values) + dot(low, values)


def kernel(
    n_inst,
    n_mp,
    migrants,
    kv_heads,
    ints,
    hidden,
    weight,
    gain,
    queries,
    pool,
    out,
    pool_v,
    hidden_v,
    weight_v,
    gain_v,
    query_v,
    stage,
    leaving,
    cache,
    part_out,
    part_in,
    key_all,
    value_all,
    in_sem,
    weight_sem,
    own_sem,
    page_send,
    page_recv,
    mig_send,
    mig_recv,
    part_send,
    part_recv,
):
    inst = lax.axis_index("inst")
    mp = lax.axis_index("mp")
    steps, requests, _ = hidden.shape
    head_dim = gain.shape[1]
    pair = 2 * head_dim
    page = pool.shape[1]
    rows = steps * requests
    portion = query_v.shape[2] // head_dim
    share = n_mp // kv_heads
    context = n_mp * page
    own_head = mp // share

    def columns(head):
        return pl.ds(pl.multiple_of(head * pair, pair), pair)

    loads = [
        pltpu.make_async_copy(pool, pool_v, in_sem.at[0]),
        pltpu.make_async_copy(hidden, hidden_v, in_sem.at[1]),
        pltpu.make_async_copy(
            queries.at[
                :,
                :,
                pl.ds(pl.multiple_of(mp * (portion * head_dim), head_dim), portion * head_dim),
            ],
            query_v,
            in_sem.at[2],
        ),
        pltpu.make_async_copy(gain, gain_v, in_sem.at[3]),
    ]
    heads = [lax.rem(own_head + 1 + j, kv_heads) for j in range(kv_heads)]
    weight_loads = [
        pltpu.make_async_copy(weight.at[:, columns(head)], weight_v.at[j], weight_sem.at[j])
        for j, head in enumerate(heads)
    ]
    loads[0].start()
    loads[1].start()
    for load in weight_loads:
        load.start()
    loads[2].start()
    loads[3].start()

    barrier = pltpu.get_barrier_semaphore()

    def greet_instance(away, to_inst):
        def greet(other):
            pl.semaphore_signal(
                barrier, inc=1, device_id={"inst": to_inst, "mp": other}, device_id_type=MESH
            )

        loop(n_mp, greet)

    def greet_peer(k):
        pl.semaphore_signal(
            barrier,
            inc=1,
            device_id={"inst": inst, "mp": lax.rem(mp + 1 + k, n_mp)},
            device_id_type=MESH,
        )

    loop(n_mp - 1, greet_peer)
    loop(n_inst - 1, lambda k: greet_instance(k, lax.rem(inst + 1 + k, n_inst)))

    table_at, length_at, dest_at = 0, requests, 2 * requests
    local_at = dest_at + n_inst * migrants
    slot_at = local_at + n_inst * migrants

    loads[0].wait()
    for r in range(requests):
        stage[r] = pool_v[ints[table_at + r]]

    def take_leaving(k):
        to_inst = lax.rem(inst + 1 + k, n_inst)
        slot = ints[slot_at]
        for u in range(1, migrants):
            slot = jnp.where(
                ints[dest_at + inst * migrants + u] == to_inst, ints[slot_at + u], slot
            )
        leaving[k] = pool_v[slot]

    loop(n_inst - 1, take_leaving)

    def page_copy(k):
        to = lax.rem(mp + 1 + k, n_mp)
        return pltpu.make_async_remote_copy(
            src_ref=stage.at[:, :, columns(to // share)],
            dst_ref=cache.at[pl.ds(0, requests), mp],
            send_sem=page_send.at[k],
            recv_sem=page_recv.at[k],
            device_id={"inst": inst, "mp": to},
            device_id_type=MESH,
        )

    def mig_copy(k, to, column):
        return pltpu.make_async_remote_copy(
            src_ref=leaving.at[k, :, columns(to // share)],
            dst_ref=cache.at[requests + k, column],
            send_sem=mig_send.at[k, to],
            recv_sem=mig_recv.at[k, column],
            device_id={"inst": lax.rem(inst + 1 + k, n_inst), "mp": to},
            device_id_type=MESH,
        )

    def part_copy(j, k):
        to = lax.rem(mp + 1 + k, n_mp)
        return pltpu.make_async_remote_copy(
            src_ref=part_out.at[j],
            dst_ref=part_in.at[k],
            send_sem=part_send.at[k],
            recv_sem=part_recv.at[k],
            device_id={"inst": inst, "mp": to},
            device_id_type=MESH,
        )

    own_copy = pltpu.make_async_copy(
        stage.at[:, :, columns(own_head)], cache.at[pl.ds(0, requests), mp], own_sem
    )
    own_copy.start()

    pl.semaphore_wait(barrier, n_inst * n_mp - 1)
    loop(n_mp - 1, lambda k: page_copy(k).start())
    loop(n_inst - 1, lambda k: loop(n_mp, lambda to: mig_copy(k, to, mp).start()))

    loads[1].wait()
    features = hidden_v[...].astype(F32).reshape(rows, hidden.shape[2]).astype(BF16)
    for j in range(kv_heads):
        weight_loads[j].wait()
        part_out[j] = dot(features, weight_v[j])
        if share == 1:
            if j < kv_heads - 1:
                part_copy(j, j).start()
    if share > 1:

        def send_part(k):
            to = lax.rem(mp + 1 + k, n_mp)
            j = lax.rem(to // share - own_head - 1 + 2 * kv_heads, kv_heads)
            part_copy(j, k).start()

        loop(n_mp - 1, send_part)

    block = [jnp.int32(r) for r in range(requests)]
    for k in range(n_inst - 1):
        source = lax.rem(inst + 2 * n_inst - 1 - k, n_inst)
        place = jnp.int32(-1)
        for u in range(migrants):
            at = source * migrants + u
            place = jnp.where(ints[dest_at + at] == inst, ints[local_at + at], place)
        for r in range(requests):
            block[r] = jnp.where(place == r, requests + k, block[r])

    row8 = lax.broadcasted_iota(jnp.int32, (requests, head_dim), 0)
    length8 = jnp.zeros((requests, head_dim), jnp.int32)
    for r in range(requests):
        length8 = jnp.where(row8 == r, ints[length_at + r], length8)

    half = head_dim // 2
    lane = lax.broadcasted_iota(jnp.int32, (rows, head_dim), 1)
    pair_index = jnp.where(lane < half, lane, lane - half)
    frequency = jnp.exp(-(2.0 * pair_index.astype(F32) / head_dim) * math.log(1000000.0))
    place = jnp.concatenate([(length8 + t).astype(F32) for t in range(steps)], axis=0)
    angle = place * frequency
    cosine = jnp.cos(angle)
    sine = jnp.sin(angle)
    sine = jnp.where(lane < half, -sine, sine)

    cached_lane = lax.broadcasted_iota(jnp.int32, (requests, requests * context), 1)
    first = lax.broadcasted_iota(jnp.int32, (requests, requests * context), 0) * context
    last = first + jnp.broadcast_to(length8[:, :1], first.shape)
    bias = jnp.where((cached_lane >= first) & (cached_lane < last), 0.0, -1e30).astype(F32)

    row = lax.broadcasted_iota(jnp.int32, (rows, 128), 0)
    column = lax.broadcasted_iota(jnp.int32, (rows, 128), 1)
    fresh_bias = jnp.where(
        (lax.rem(row, requests) == lax.rem(column, requests)) & (column <= row), 0.0, -1e30
    ).astype(F32)

    loads[2].wait()
    query = jnp.concatenate(
        [
            query_v[t, :, g * head_dim : (g + 1) * head_dim].astype(F32)
            for g in range(portion)
            for t in range(steps)
        ],
        axis=0,
    ).astype(BF16)
    value_all[:, head_dim:] = jnp.ones((requests * context, head_dim), BF16)
    scale = 1.0 / math.sqrt(head_dim)

    own_copy.wait()
    loop(n_mp - 1, lambda k: page_copy(k).wait_recv())
    loop(n_inst - 1, lambda k: loop(n_mp, lambda to: mig_copy(k, to, to).wait_recv()))
    for r in range(requests):
        held = cache[block[r]].reshape(context, pair)
        key_all[r * context : (r + 1) * context, :] = held[:, :head_dim]
        value_all[r * context : (r + 1) * context, :head_dim] = held[:, head_dim:]

    total_rows = portion * rows
    scores = dot(query, key_all[...], ((1,), (1,))) * scale
    scores = scores.reshape(portion * steps, requests, requests * context) + bias[None]
    scores = scores.reshape(total_rows, requests * context)
    peak = jnp.max(scores, axis=-1, keepdims=True)
    summed = weighted(jnp.exp(scores - peak), value_all[...])

    loads[3].wait()
    loop(n_mp - 1, lambda k: part_copy(0, k).wait_recv())
    projected = part_out[kv_heads - 1]
    for k in range(n_mp - 1):
        projected = projected + part_in[k]
    keys = projected[:, :head_dim]
    factor = lax.rsqrt(jnp.mean(keys * keys, axis=-1, keepdims=True) + 1e-06)
    keys = keys * factor * gain_v[...]
    keys = keys * cosine + pltpu.roll(keys, half, 1) * sine
    blank = jnp.zeros((128 - rows, head_dim), F32)
    fresh_keys = jnp.concatenate([keys, blank], axis=0).astype(BF16)
    fresh_values = jnp.concatenate([projected[:, head_dim:], blank], axis=0).astype(BF16)
    fresh_values = jnp.concatenate(
        [fresh_values, jnp.ones((128, head_dim), BF16)], axis=1
    )
    fresh = dot(query, fresh_keys, ((1,), (1,))) * scale
    fresh = (fresh.reshape(portion, rows, 128) + fresh_bias[None]).reshape(total_rows, 128)
    highest = jnp.maximum(peak, jnp.max(fresh, axis=-1, keepdims=True))
    summed = summed * jnp.exp(peak - highest) + weighted(jnp.exp(fresh - highest), fresh_values)
    result = summed[:, :head_dim] / summed[:, head_dim:]
    for t in range(steps):
        for g in range(portion):
            at = (g * steps + t) * requests
            out[t, :, g * head_dim : (g + 1) * head_dim] = result[at : at + requests].astype(BF16)

    loop(n_mp - 1, lambda k: page_copy(k).wait_send())
    loop(n_inst - 1, lambda k: loop(n_mp, lambda to: mig_copy(k, to, mp).wait_send()))
    loop(n_mp - 1, lambda k: part_copy(0, k).wait_send())


def local(
    n_inst,
    n_mp,
    hidden_states,
    kv_weight,
    key_gain,
    queries,
    kv_pool,
    page_table,
    lengths,
    mig_dest,
    mig_local,
    mig_slots,
):
    steps, requests, depth = hidden_states.shape
    head_dim = key_gain.shape[0]
    width = kv_weight.shape[1]
    pair = 2 * head_dim
    kv_heads = width // pair
    portion = queries.shape[2] // n_mp
    migrants = mig_dest.shape[1]
    pool = kv_pool[0]
    page = pool.shape[1]
    rows = steps * requests
    context = n_mp * page
    assert page_table.shape[1] == 1 and n_mp % kv_heads == 0
    ints = jnp.concatenate(
        [
            page_table.reshape(-1),
            lengths,
            mig_dest.reshape(-1),
            mig_local.reshape(-1),
            mig_slots.reshape(-1),
        ]
    )
    anywhere = pl.BlockSpec(memory_space=pl.ANY)
    return pl.pallas_call(
        functools.partial(kernel, n_inst, n_mp, migrants, kv_heads),
        out_shape=jax.ShapeDtypeStruct((steps, requests, portion), BF16),
        in_specs=[pl.BlockSpec(memory_space=pltpu.SMEM)] + [anywhere] * 5,
        out_specs=pl.BlockSpec(memory_space=pltpu.VMEM),
        scratch_shapes=[
            pltpu.VMEM(pool.shape, BF16),
            pltpu.VMEM(hidden_states.shape, BF16),
            pltpu.VMEM((kv_heads, depth, pair), BF16),
            pltpu.VMEM((1, head_dim), F32),
            pltpu.VMEM((steps, requests, portion), BF16),
            pltpu.VMEM((requests, page, width), BF16),
            pltpu.VMEM((n_inst - 1, page, width), BF16),
            pltpu.VMEM((requests + n_inst - 1, n_mp, page, pair), BF16),
            pltpu.VMEM((kv_heads, rows, pair), F32),
            pltpu.VMEM((n_mp - 1, rows, pair), F32),
            pltpu.VMEM((requests * context, head_dim), BF16),
            pltpu.VMEM((requests * context, pair), BF16),
            pltpu.SemaphoreType.DMA((4,)),
            pltpu.SemaphoreType.DMA((kv_heads,)),
            pltpu.SemaphoreType.DMA,
            pltpu.SemaphoreType.DMA((n_mp - 1,)),
            pltpu.SemaphoreType.DMA((n_mp - 1,)),
            pltpu.SemaphoreType.DMA((n_inst - 1, n_mp)),
            pltpu.SemaphoreType.DMA((n_inst - 1, n_mp)),
            pltpu.SemaphoreType.DMA((n_mp - 1,)),
            pltpu.SemaphoreType.DMA((n_mp - 1,)),
        ],
        compiler_params=pltpu.CompilerParams(
            collective_id=0, has_side_effects=True, vmem_limit_bytes=32 * 1024 * 1024
        ),
    )(ints, hidden_states, kv_weight, key_gain.reshape(1, head_dim), queries, pool)


def solution(mesh):
    placed = (
        P(None, ("groups", "inst"), "mp"),
        P("mp", None),
        P(),
        P(None, ("groups", "inst"), None),
        P(("groups", "inst"), "mp", None, None),
        P(("groups", "inst"), None, "mp"),
        P(("groups", "inst")),
        P("groups", None),
        P("groups", None),
        P(("groups", "inst"), None, None, "mp"),
    )
    return jax.shard_map(
        functools.partial(local, mesh.shape["inst"], mesh.shape["mp"]),
        mesh=mesh,
        in_specs=placed,
        out_specs=P(None, ("groups", "inst"), "mp"),
        check_vma=False,
    )
```

time: 84.7 us -> 22.8 us (0.27)
  waiting for transfers between devices: 20.6 us -> 0 us
  blocking collectives: 16.3 us -> 0 us
  Pallas kernels: 0 us -> 14.2 us
  between operations: 13.7 us -> 0.02 us
  starting transfers between devices: 9.98 us -> 0 us
  other arithmetic: 6.75 us -> 0 us
  local copies, waits for them, and re-layouts: 13.9 us -> 8.21 us
  matrix products: 2.82 us -> 0 us
    all_gather x1 -> x0, blocking collectives: 16.3 us -> none  [local(): lax.all_gather(leaving, 'inst', axis=0, tiled=True)]
    pallas_call x0 -> x1, Pallas kernels: none -> 14.2 us  [local(): pl.pallas_call(functools.partial(kernel, n_inst, n_mp, migrants, kv_heads...]
    all_to_all x3 -> x0, waiting for transfers between devices: 10.4 us -> none  [the longest x1 6.56 us: local(): lax.all_to_all(summed, 'mp', split_axis=2, concat_axis=2, tiled=True)]
    psum x1 -> x0, waiting for transfers between devices: 10.2 us -> none  [local(): lax.psum(partial_sum, 'mp').reshape(steps, requests, kv_heads, 2, head_dim)]
    all_to_all x3 -> x0, starting transfers between devices: 9.94 us -> none  [the longest x1 3.46 us: local(): lax.all_to_all(summed, 'mp', split_axis=2, concat_axis=2, tiled=True)]
    dot_general x3 -> x0, matrix products: 2.82 us -> none  [the longest x1 1.93 us: local(): jnp.einsum('trd,dc->trc', hidden_states, kv_weight, preferred_element_typ...]
    gather x4 -> x0, local copies, waits for them, and re-layouts: 2.62 us -> none  [the longest x1 0.74 us: local(): slot_index = table[jnp.arange(requests)[None, :], deeper]]
    unnamed x26 -> x13, local copies, waits for them, and re-layouts: 4.75 us -> 7.27 us
  transfers between devices with their start and end apart: 4 -> 0, of which waited for: 4 -> 0; matrix products, arithmetic and copies ran while one was open for 14% -> 0% of each run, Pallas kernels for 0% -> 0%
where the time goes in v1:
time: 22.8 us; the launch traced here: 22.5 us
  Pallas kernels  14.2 us (62%)
  local copies, waits for them, and re-layouts  8.21 us (36%)
    pallas_call x1, Pallas kernels, local(): pl.pallas_call(functools.partial(kernel, n_inst, n_mp, migrants, kv_heads...  14.2 us
    unnamed x13, local copies, waits for them, and re-layouts  7.27 us
    concatenate x1, local copies, waits for them, and re-layouts, local(): jnp.concatenate([page_table.reshape(-1), lengths, mig_dest.reshape(-1), m...  0.76 us

profile of v1, /device:TPU:0, one launch (start us, length us, event | category | flops | bytes accessed | tf_op | source)
XLA Modules:
  0.0 22.5 jit_solution(9150076811957707790)
XLA Ops:
  0.0 0.8 %copy.13 = s32[4,2]{1,0:T(4,128)S(1)} copy(s32[4,2]{0,1:T(2,128)} %param.17) | data formatting | bytes 64 | tf_op args[7]
  0.8 0.1 reshape.16
  0.9 0.8 %copy.14 = s32[4,2]{1,0:T(4,128)S(1)} copy(s32[4,2]{0,1:T(2,128)} %param.18) | data formatting | bytes 64 | tf_op args[8]
  1.6 0.1 reshape.17
  1.7 0.8 %concatenate.3.ints = s32[34]{0:T(128)S(1)} concatenate(s32[8]{0:T(128)} %bitcast.6, s32[8]{0:T(128)} %param.16, s32[8]{0:T(128)S(1)} %reshape.16, s32[8]{0:T(128)S(1)} %reshape.17, s32[2]{0:T(128)} %bitcast.7), dimensions={0} | concatenate | bytes 272 | tf_op jit(solution)/shard_map/concatenate | solution.py:326
  2.5 0.0 copy-start
  2.5 1.7 %copy-done = bf16[1280,1024]{1,0:T(8,128)(2,1)S(1)} copy-done((bf16[1280,1024]{1,0:T(8,128)(2,1)S(1)}, bf16[1280,1024]{1,0:T(8,128)(2,1)}, u32[]{:S(2)}) %copy-start) | copy-done | bytes 2621464
  4.2 0.0 copy-start.1
  4.2 1.0 %copy-done.1 = bf16[1,10,16,1024]{3,2,1,0:T(8,128)(2,1)S(1)} copy-done((bf16[1,10,16,1024]{3,2,1,0:T(8,128)(2,1)S(1)}, bf16[1,10,16,1024]{3,2,1,0:T(8,128)(2,1)}, u32[]{:S(2)}) %copy-start.1) | copy-done | bytes 327704
  5.2 0.0 copy-start.2
  5.2 0.9 %copy-done.2 = bf16[3,8,4096]{2,1,0:T(8,128)(2,1)S(1)} copy-done((bf16[3,8,4096]{2,1,0:T(8,128)(2,1)S(1)}, bf16[3,8,4096]{2,1,0:T(8,128)(2,1)}, u32[]{:S(2)}) %copy-start.2) | copy-done | bytes 196632
  6.1 0.0 copy-start.3
  6.1 0.8 %copy-done.3 = bf16[3,8,1280]{2,1,0:T(8,128)(2,1)S(1)} copy-done((bf16[3,8,1280]{2,1,0:T(8,128)(2,1)S(1)}, bf16[3,8,1280]{2,1,0:T(8,128)(2,1)}, u32[]{:S(2)}) %copy-start.3) | copy-done | bytes 61464
  6.9 0.0 copy-start.4
  6.9 0.7 %copy-done.4 = f32[128]{0:T(128)S(1)} copy-done((f32[128]{0:T(128)S(1)}, f32[128]{0:T(128)}, u32[]{:S(2)}) %copy-start.4) | copy-done | bytes 536
  7.6 14.2 %shard_map.100 = bf16[3,8,1024]{2,1,0:T(8,128)(2,1)S(1)} custom-call(s32[34]{0:T(128)S(1)} %concatenate.3.ints, bf16[3,8,1280]{2,1,0:T(8,128)(2,1)S(1)} %copy-done.3, bf16[1280,1024]{1,0:T(8,128)(2,1)S(1)} %copy-done, f32[1,128]{1,0:T(1,128)S(1)} %bitcast.5, bf16[3,8,4096]{2,1,0:T(8,128)(2,1)S(1)} %copy-done.2, bf16[10,16,1024]{2,1,0:T(8,128)(2,1)S(1)} %bitcast.4), custom_call_target="tpu_custom_call" | custom-call | tf_op jit(solution)/shard_map/pallas_call | solution.py:336
  21.8 0.6 %copy.16 = bf16[3,8,1024]{2,1,0:T(8,128)(2,1)} copy(bf16[3,8,1024]{2,1,0:T(8,128)(2,1)S(1)} %shard_map.100) | data formatting | bytes 98304
Async XLA Ops:
  2.5 1.7 %copy-start = (bf16[1280,1024]{1,0:T(8,128)(2,1)S(1)}, bf16[1280,1024]{1,0:T(8,128)(2,1)}, u32[]{:S(2)}) copy-start(bf16[1280,1024]{1,0:T(8,128)(2,1)} %weight.1) | copy-start | bytes 7864324
  4.2 1.0 %copy-start.1 = (bf16[1,10,16,1024]{3,2,1,0:T(8,128)(2,1)S(1)}, bf16[1,10,16,1024]{3,2,1,0:T(8,128)(2,1)}, u32[]{:S(2)}) copy-start(bf16[1,10,16,1024]{3,2,1,0:T(8,128)(2,1)} %param.14) | copy-start | bytes 983044
  5.2 0.9 %copy-start.2 = (bf16[3,8,4096]{2,1,0:T(8,128)(2,1)S(1)}, bf16[3,8,4096]{2,1,0:T(8,128)(2,1)}, u32[]{:S(2)}) copy-start(bf16[3,8,4096]{2,1,0:T(8,128)(2,1)} %queries.1) | copy-start | bytes 589828
  6.1 0.8 %copy-start.3 = (bf16[3,8,1280]{2,1,0:T(8,128)(2,1)S(1)}, bf16[3,8,1280]{2,1,0:T(8,128)(2,1)}, u32[]{:S(2)}) copy-start(bf16[3,8,1280]{2,1,0:T(8,128)(2,1)} %hidden.1) | copy-start | bytes 184324
  6.9 0.7 %copy-start.4 = (f32[128]{0:T(128)S(1)}, f32[128]{0:T(128)}, u32[]{:S(2)}) copy-start(f32[128]{0:T(128)} %param.12) | copy-start | bytes 1540

commit v2 on v1

--- a/solution.py
+++ b/solution.py
@@ -36,7 +36,11 @@
     n_mp,
     migrants,
     kv_heads,
-    ints,
+    table_h,
+    length_h,
+    dest_h,
+    local_h,
+    slot_h,
     hidden,
     weight,
     gain,
@@ -55,6 +59,12 @@
     part_in,
     key_all,
     value_all,
+    table,
+    length,
+    mig_dest,
+    mig_local,
+    mig_slot,
+    int_sem,
     in_sem,
     weight_sem,
     own_sem,
@@ -99,7 +109,21 @@
         pltpu.make_async_copy(weight.at[:, columns(head)], weight_v.at[j], weight_sem.at[j])
         for j, head in enumerate(heads)
     ]
+    int_loads = [
+        pltpu.make_async_copy(source, target, int_sem.at[n])
+        for n, (source, target) in enumerate(
+            [
+                (table_h, table),
+                (slot_h, mig_slot),
+                (dest_h, mig_dest),
+                (local_h, mig_local),
+                (length_h, length),
+            ]
+        )
+    ]
     loads[0].start()
+    for load in int_loads:
+        load.start()
     loads[1].start()
     for load in weight_loads:
         load.start()
@@ -127,21 +151,17 @@
     loop(n_mp - 1, greet_peer)
     loop(n_inst - 1, lambda k: greet_instance(k, lax.rem(inst + 1 + k, n_inst)))
 
-    table_at, length_at, dest_at = 0, requests, 2 * requests
-    local_at = dest_at + n_inst * migrants
-    slot_at = local_at + n_inst * migrants
-
+    for load in int_loads:
+        load.wait()
     loads[0].wait()
     for r in range(requests):
-        stage[r] = pool_v[ints[table_at + r]]
+        stage[r] = pool_v[table[r]]
 
     def take_leaving(k):
         to_inst = lax.rem(inst + 1 + k, n_inst)
-        slot = ints[slot_at]
+        slot = mig_slot[0]
         for u in range(1, migrants):
-            slot = jnp.where(
-                ints[dest_at + inst * migrants + u] == to_inst, ints[slot_at + u], slot
-            )
+            slot = jnp.where(mig_dest[u, inst] == to_inst, mig_slot[u], slot)
         leaving[k] = pool_v[slot]
 
     loop(n_inst - 1, take_leaving)
@@ -209,15 +229,14 @@
         source = lax.rem(inst + 2 * n_inst - 1 - k, n_inst)
         place = jnp.int32(-1)
         for u in range(migrants):
-            at = source * migrants + u
-            place = jnp.where(ints[dest_at + at] == inst, ints[local_at + at], place)
+            place = jnp.where(mig_dest[u, source] == inst, mig_local[u, source], place)
         for r in range(requests):
             block[r] = jnp.where(place == r, requests + k, block[r])
 
     row8 = lax.broadcasted_iota(jnp.int32, (requests, head_dim), 0)
     length8 = jnp.zeros((requests, head_dim), jnp.int32)
     for r in range(requests):
-        length8 = jnp.where(row8 == r, ints[length_at + r], length8)
+        length8 = jnp.where(row8 == r, length[r], length8)
 
     half = head_dim // 2
     lane = lax.broadcasted_iota(jnp.int32, (rows, head_dim), 1)
@@ -323,20 +342,11 @@
     rows = steps * requests
     context = n_mp * page
     assert page_table.shape[1] == 1 and n_mp % kv_heads == 0
-    ints = jnp.concatenate(
-        [
-            page_table.reshape(-1),
-            lengths,
-            mig_dest.reshape(-1),
-            mig_local.reshape(-1),
-            mig_slots.reshape(-1),
-        ]
-    )
-    anywhere = pl.BlockSpec(memory_space=pl.ANY)
+    far = pl.BlockSpec(memory_space=pltpu.HBM)
     return pl.pallas_call(
         functools.partial(kernel, n_inst, n_mp, migrants, kv_heads),
         out_shape=jax.ShapeDtypeStruct((steps, requests, portion), BF16),
-        in_specs=[pl.BlockSpec(memory_space=pltpu.SMEM)] + [anywhere] * 5,
+        in_specs=[far] * 10,
         out_specs=pl.BlockSpec(memory_space=pltpu.VMEM),
         scratch_shapes=[
             pltpu.VMEM(pool.shape, BF16),
@@ -351,6 +361,12 @@
             pltpu.VMEM((n_mp - 1, rows, pair), F32),
             pltpu.VMEM((requests * context, head_dim), BF16),
             pltpu.VMEM((requests * context, pair), BF16),
+            pltpu.SMEM((requests,), jnp.int32),
+            pltpu.SMEM((requests,), jnp.int32),
+            pltpu.SMEM((migrants, n_inst), jnp.int32),
+            pltpu.SMEM((migrants, n_inst), jnp.int32),
+            pltpu.SMEM((migrants,), jnp.int32),
+            pltpu.SemaphoreType.DMA((5,)),
             pltpu.SemaphoreType.DMA((4,)),
             pltpu.SemaphoreType.DMA((kv_heads,)),
             pltpu.SemaphoreType.DMA,
@@ -364,7 +380,18 @@
         compiler_params=pltpu.CompilerParams(
             collective_id=0, has_side_effects=True, vmem_limit_bytes=32 * 1024 * 1024
         ),
-    )(ints, hidden_states, kv_weight, key_gain.reshape(1, head_dim), queries, pool)
+    )(
+        page_table.reshape(-1),
+        lengths,
+        mig_dest.T,
+        mig_local.T,
+        mig_slots.reshape(-1),
+        hidden_states,
+        kv_weight,
+        key_gain.reshape(1, head_dim),
+        queries,
+        pool,
+    )
 
 
 def solution(mesh):

time: 22.8 us -> 23.1 us (1.013)
  local copies, waits for them, and re-layouts: 8.21 us -> 9.06 us
  Pallas kernels: 14.2 us -> 13.7 us
    unnamed x13 -> x21, local copies, waits for them, and re-layouts: 7.27 us -> 9.06 us
    concatenate x1 -> x0, local copies, waits for them, and re-layouts: 0.76 us -> none  [local(): jnp.concatenate([page_table.reshape(-1), lengths, mig_dest.reshape(-1), m...]
    pallas_call x1, Pallas kernels: 14.2 us -> 13.7 us  [local(): pl.pallas_call(functools.partial(kernel, n_inst, n_mp, migrants, kv_heads...]
where the time goes in v2:
time: 23.1 us; the launch traced here: 22.8 us
  Pallas kernels  13.7 us (59%)
  local copies, waits for them, and re-layouts  9.06 us (39%)
    pallas_call x1, Pallas kernels, local(): pl.pallas_call(functools.partial(kernel, n_inst, n_mp, migrants, kv_heads...  13.7 us
    unnamed x21, local copies, waits for them, and re-layouts  9.06 us

profile of v2, /device:TPU:0, one launch (start us, length us, event | category | flops | bytes accessed | tf_op | source)
XLA Modules:
  0.0 22.8 jit_solution(11689760001066497005)
XLA Ops:
  0.0 0.0 copy-start
  0.0 1.7 %copy-done = bf16[1280,1024]{1,0:T(8,128)(2,1)S(1)} copy-done((bf16[1280,1024]{1,0:T(8,128)(2,1)S(1)}, bf16[1280,1024]{1,0:T(8,128)(2,1)}, u32[]{:S(2)}) %copy-start) | copy-done | bytes 2621464
  1.7 0.0 copy-start.1
  1.7 1.0 %copy-done.1 = bf16[1,10,16,1024]{3,2,1,0:T(8,128)(2,1)S(1)} copy-done((bf16[1,10,16,1024]{3,2,1,0:T(8,128)(2,1)S(1)}, bf16[1,10,16,1024]{3,2,1,0:T(8,128)(2,1)}, u32[]{:S(2)}) %copy-start.1) | copy-done | bytes 327704
  2.7 0.0 copy-start.2
  2.7 0.9 %copy-done.2 = bf16[3,8,4096]{2,1,0:T(8,128)(2,1)S(1)} copy-done((bf16[3,8,4096]{2,1,0:T(8,128)(2,1)S(1)}, bf16[3,8,4096]{2,1,0:T(8,128)(2,1)}, u32[]{:S(2)}) %copy-start.2) | copy-done | bytes 196632
  3.6 0.0 copy-start.3
  3.6 0.8 %copy-done.3 = bf16[3,8,1280]{2,1,0:T(8,128)(2,1)S(1)} copy-done((bf16[3,8,1280]{2,1,0:T(8,128)(2,1)S(1)}, bf16[3,8,1280]{2,1,0:T(8,128)(2,1)}, u32[]{:S(2)}) %copy-start.3) | copy-done | bytes 61464
  4.5 0.0 copy-start.4
  4.5 0.7 %copy-done.4 = s32[4,2]{0,1:T(2,128)S(1)} copy-done((s32[4,2]{0,1:T(2,128)S(1)}, s32[4,2]{0,1:T(2,128)}, u32[]{:S(2)}) %copy-start.4) | copy-done | bytes 56
  5.2 0.0 copy-start.5
  5.2 0.7 %copy-done.5 = s32[4,2]{0,1:T(2,128)S(1)} copy-done((s32[4,2]{0,1:T(2,128)S(1)}, s32[4,2]{0,1:T(2,128)}, u32[]{:S(2)}) %copy-start.5) | copy-done | bytes 56
  5.8 0.0 copy-start.6
  5.8 0.7 %copy-done.6 = s32[8,1,1]{0,2,1:T(1,128)S(1)} copy-done((s32[8,1,1]{0,2,1:T(1,128)S(1)}, s32[8,1,1]{0,2,1:T(1,128)}, u32[]{:S(2)}) %copy-start.6) | copy-done | bytes 56
  6.5 0.0 copy-start.7
  6.5 0.7 %copy-done.7 = s32[8]{0:T(128)S(1)} copy-done((s32[8]{0:T(128)S(1)}, s32[8]{0:T(128)}, u32[]{:S(2)}) %copy-start.7) | copy-done | bytes 56
  7.1 0.0 copy-start.8
  7.1 0.7 %copy-done.8 = s32[1,2,1,1]{1,3,2,0:T(1,128)S(1)} copy-done((s32[1,2,1,1]{1,3,2,0:T(1,128)S(1)}, s32[1,2,1,1]{1,3,2,0:T(1,128)}, u32[]{:S(2)}) %copy-start.8) | copy-done | bytes 32
  7.8 0.0 copy-start.9
  7.8 0.7 %copy-done.9 = f32[128]{0:T(128)S(1)} copy-done((f32[128]{0:T(128)S(1)}, f32[128]{0:T(128)}, u32[]{:S(2)}) %copy-start.9) | copy-done | bytes 536
  8.5 13.7 %shard_map.100 = bf16[3,8,1024]{2,1,0:T(8,128)(2,1)S(1)} custom-call(s32[8]{0:T(128)S(1)} %bitcast.9, s32[8]{0:T(128)S(1)} %copy-done.7, s32[2,4]{1,0:T(2,128)S(1)} %bitcast.7, s32[2,4]{1,0:T(2,128)S(1)} %bitcast.8, s32[2]{0:T(128)S(1)} %bitcast.10, bf16[3,8,1280]{2,1,0:T(8,128)(2,1)S(1)} %copy-done.3, bf16[1280,1024]{1,0:T(8,128)(2,1)S(1)} %copy-done, ...), custom_call_target="tpu_custom_call" | custom-call | tf_op jit(solution)/shard_map/pallas_call | solution.py:346
  22.2 0.6 %copy.12 = bf16[3,8,1024]{2,1,0:T(8,128)(2,1)} copy(bf16[3,8,1024]{2,1,0:T(8,128)(2,1)S(1)} %shard_map.100) | data formatting | bytes 98304
Async XLA Ops:
  0.0 1.7 %copy-start = (bf16[1280,1024]{1,0:T(8,128)(2,1)S(1)}, bf16[1280,1024]{1,0:T(8,128)(2,1)}, u32[]{:S(2)}) copy-start(bf16[1280,1024]{1,0:T(8,128)(2,1)} %weight.1) | copy-start | bytes 7864324
  1.7 1.0 %copy-start.1 = (bf16[1,10,16,1024]{3,2,1,0:T(8,128)(2,1)S(1)}, bf16[1,10,16,1024]{3,2,1,0:T(8,128)(2,1)}, u32[]{:S(2)}) copy-start(bf16[1,10,16,1024]{3,2,1,0:T(8,128)(2,1)} %param.14) | copy-start | bytes 983044
  2.7 0.9 %copy-start.2 = (bf16[3,8,4096]{2,1,0:T(8,128)(2,1)S(1)}, bf16[3,8,4096]{2,1,0:T(8,128)(2,1)}, u32[]{:S(2)}) copy-start(bf16[3,8,4096]{2,1,0:T(8,128)(2,1)} %queries.1) | copy-start | bytes 589828
  3.6 0.8 %copy-start.3 = (bf16[3,8,1280]{2,1,0:T(8,128)(2,1)S(1)}, bf16[3,8,1280]{2,1,0:T(8,128)(2,1)}, u32[]{:S(2)}) copy-start(bf16[3,8,1280]{2,1,0:T(8,128)(2,1)} %hidden.1) | copy-start | bytes 184324
  4.5 0.7 %copy-start.4 = (s32[4,2]{0,1:T(2,128)S(1)}, s32[4,2]{0,1:T(2,128)}, u32[]{:S(2)}) copy-start(s32[4,2]{0,1:T(2,128)} %param.17) | copy-start | bytes 100
  5.2 0.7 %copy-start.5 = (s32[4,2]{0,1:T(2,128)S(1)}, s32[4,2]{0,1:T(2,128)}, u32[]{:S(2)}) copy-start(s32[4,2]{0,1:T(2,128)} %param.18) | copy-start | bytes 100
  5.8 0.7 %copy-start.6 = (s32[8,1,1]{0,2,1:T(1,128)S(1)}, s32[8,1,1]{0,2,1:T(1,128)}, u32[]{:S(2)}) copy-start(s32[8,1,1]{0,2,1:T(1,128)} %param.15) | copy-start | bytes 100
  6.5 0.7 %copy-start.7 = (s32[8]{0:T(128)S(1)}, s32[8]{0:T(128)}, u32[]{:S(2)}) copy-start(s32[8]{0:T(128)} %length_h.1) | copy-start | bytes 100
  7.1 0.7 %copy-start.8 = (s32[1,2,1,1]{1,3,2,0:T(1,128)S(1)}, s32[1,2,1,1]{1,3,2,0:T(1,128)}, u32[]{:S(2)}) copy-start(s32[1,2,1,1]{1,3,2,0:T(1,128)} %param.19) | copy-start | bytes 28
  7.8 0.7 %copy-start.9 = (f32[128]{0:T(128)S(1)}, f32[128]{0:T(128)}, u32[]{:S(2)}) copy-start(f32[128]{0:T(128)} %param.12) | copy-start | bytes 1540

commit v3 on v2

--- a/solution.py
+++ b/solution.py
@@ -378,7 +378,7 @@
             pltpu.SemaphoreType.DMA((n_mp - 1,)),
         ],
         compiler_params=pltpu.CompilerParams(
-            collective_id=0, has_side_effects=True, vmem_limit_bytes=32 * 1024 * 1024
+            collective_id=0, has_side_effects=True, vmem_limit_bytes=60 * 1024 * 1024
         ),
     )(
         page_table.reshape(-1),

time: 23.1 us -> 15.4 us (0.67)
  local copies, waits for them, and re-layouts: 9.06 us -> 1.42 us
    unnamed x21 -> x1, local copies, waits for them, and re-layouts: 9.06 us -> 1.42 us
where the time goes in v3:
time: 15.4 us; the launch traced here: 15.2 us
  Pallas kernels  13.8 us (90%)
  local copies, waits for them, and re-layouts  1.42 us (9%)
    pallas_call x1, Pallas kernels, local(): pl.pallas_call(functools.partial(kernel, n_inst, n_mp, migrants, kv_heads...  13.8 us
    unnamed x1, local copies, waits for them, and re-layouts  1.42 us

profile of v3, /device:TPU:0, one launch (start us, length us, event | category | flops | bytes accessed | tf_op | source)
XLA Modules:
  0.0 15.2 jit_solution(17659050718132706287)
XLA Ops:
  0.0 13.8 %shard_map.100 = bf16[3,8,1024]{2,1,0:T(8,128)(2,1)} custom-call(s32[8]{0:T(128)} %bitcast.9, s32[8]{0:T(128)} %length_h.1, s32[2,4]{1,0:T(2,128)} %bitcast.7, s32[2,4]{1,0:T(2,128)} %bitcast.8, s32[2]{0:T(128)} %bitcast.10, bf16[3,8,1280]{2,1,0:T(8,128)(2,1)} %hidden.1, bf16[1280,1024]{1,0:T(8,128)(2,1)} %weight.1, f32[1,128]{1,0:T(1,128)} %bitcast.11, ...), custom_call_target="tpu_custom_call" | custom-call | tf_op jit(solution)/shard_map/pallas_call | solution.py:346
  13.8 1.4 %copy.12 = bf16[3,8,1024]{2,1,0:T(8,128)(2,1)} copy(bf16[3,8,1024]{2,1,0:T(8,128)(2,1)} %shard_map.100) | data formatting | bytes 98304

commit v4 on v2

--- a/solution.py
+++ b/solution.py
@@ -381,16 +381,21 @@
             collective_id=0, has_side_effects=True, vmem_limit_bytes=32 * 1024 * 1024
         ),
     )(
-        page_table.reshape(-1),
-        lengths,
-        mig_dest.T,
-        mig_local.T,
-        mig_slots.reshape(-1),
-        hidden_states,
-        kv_weight,
-        key_gain.reshape(1, head_dim),
-        queries,
-        pool,
+        *[
+            pltpu.with_memory_space_constraint(operand, pltpu.HBM)
+            for operand in (
+                page_table.reshape(-1),
+                lengths,
+                mig_dest.T,
+                mig_local.T,
+                mig_slots.reshape(-1),
+                hidden_states,
+                kv_weight,
+                key_gain.reshape(1, head_dim),
+                queries,
+                pool,
+            )
+        ]
     )
 
 

time: 23.1 us -> 14 us (0.61)
  local copies, waits for them, and re-layouts: 9.06 us -> 0.62 us
  Pallas kernels: 13.7 us -> 13.2 us
    unnamed x21 -> x1, local copies, waits for them, and re-layouts: 9.06 us -> 0.62 us
    pallas_call x1, Pallas kernels: 13.7 us -> 13.2 us  [local(): pl.pallas_call(functools.partial(kernel, n_inst, n_mp, migrants, kv_heads...]
where the time goes in v4:
time: 14 us; the launch traced here: 13.8 us
  Pallas kernels  13.2 us (94%)
  local copies, waits for them, and re-layouts  0.62 us (4%)
    pallas_call x1, Pallas kernels, local(): pl.pallas_call(functools.partial(kernel, n_inst, n_mp, migrants, kv_heads...  13.2 us
    unnamed x1, local copies, waits for them, and re-layouts  0.62 us

profile of v4, /device:TPU:0, one launch (start us, length us, event | category | flops | bytes accessed | tf_op | source)
XLA Modules:
  0.0 13.8 jit_solution(5304333365865656272)
XLA Ops:
  0.0 13.2 %shard_map.100 = bf16[3,8,1024]{2,1,0:T(8,128)(2,1)S(1)} custom-call(s32[8]{0:T(128)} %bitcast.9, s32[8]{0:T(128)} %length_h.1, s32[2,4]{1,0:T(2,128)} %bitcast.7, s32[2,4]{1,0:T(2,128)} %bitcast.8, s32[2]{0:T(128)} %bitcast.10, bf16[3,8,1280]{2,1,0:T(8,128)(2,1)} %hidden.1, bf16[1280,1024]{1,0:T(8,128)(2,1)} %weight.1, f32[1,128]{1,0:T(1,128)} %bitcast.11, ...), custom_call_target="tpu_custom_call" | custom-call | tf_op jit(solution)/shard_map/pallas_call | solution.py:346
  13.2 0.6 %copy.12 = bf16[3,8,1024]{2,1,0:T(8,128)(2,1)} copy(bf16[3,8,1024]{2,1,0:T(8,128)(2,1)S(1)} %shard_map.100) | data formatting | bytes 98304

commit v5 on v4

--- a/solution.py
+++ b/solution.py
@@ -55,10 +55,11 @@
     stage,
     leaving,
     cache,
+    outgoing,
+    passing,
+    arrived,
     part_out,
     part_in,
-    key_all,
-    value_all,
     table,
     length,
     mig_dest,
@@ -70,8 +71,10 @@
     own_sem,
     page_send,
     page_recv,
-    mig_send,
-    mig_recv,
+    leave_send,
+    leave_recv,
+    hop_send,
+    hop_recv,
     part_send,
     part_recv,
 ):
@@ -132,14 +135,6 @@
 
     barrier = pltpu.get_barrier_semaphore()
 
-    def greet_instance(away, to_inst):
-        def greet(other):
-            pl.semaphore_signal(
-                barrier, inc=1, device_id={"inst": to_inst, "mp": other}, device_id_type=MESH
-            )
-
-        loop(n_mp, greet)
-
     def greet_peer(k):
         pl.semaphore_signal(
             barrier,
@@ -149,7 +144,17 @@
         )
 
     loop(n_mp - 1, greet_peer)
-    loop(n_inst - 1, lambda k: greet_instance(k, lax.rem(inst + 1 + k, n_inst)))
+    for away, there in ((1, inst < n_inst - 1), (-1, inst > 0)):
+
+        @pl.when(there)
+        def _():
+            pl.semaphore_signal(
+                barrier, inc=1, device_id={"inst": inst + away, "mp": mp}, device_id_type=MESH
+            )
+
+    greetings = (
+        n_mp - 1 + jnp.where(inst < n_inst - 1, 1, 0) + jnp.where(inst > 0, 1, 0)
+    )
 
     for load in int_loads:
         load.wait()
@@ -158,7 +163,7 @@
         stage[r] = pool_v[table[r]]
 
     def take_leaving(k):
-        to_inst = lax.rem(inst + 1 + k, n_inst)
+        to_inst = jnp.where(k < inst, k, k + 1)
         slot = mig_slot[0]
         for u in range(1, migrants):
             slot = jnp.where(mig_dest[u, inst] == to_inst, mig_slot[u], slot)
@@ -177,15 +182,70 @@
             device_id_type=MESH,
         )
 
-    def mig_copy(k, to, column):
+    def leave_copy(k):
+        to = lax.rem(mp + 1 + k, n_mp)
         return pltpu.make_async_remote_copy(
-            src_ref=leaving.at[k, :, columns(to // share)],
-            dst_ref=cache.at[requests + k, column],
-            send_sem=mig_send.at[k, to],
-            recv_sem=mig_recv.at[k, column],
-            device_id={"inst": lax.rem(inst + 1 + k, n_inst), "mp": to},
+            src_ref=leaving.at[:, :, columns(to // share)],
+            dst_ref=outgoing.at[:, mp],
+            send_sem=leave_send.at[k],
+            recv_sem=leave_recv.at[k],
+            device_id={"inst": inst, "mp": to},
             device_id_type=MESH,
         )
+
+    def line(way):
+        return inst if way == 0 else n_inst - 1 - inst
+
+    def sends(way, hop, rest):
+        return (line(way) >= hop - 1) & (line(way) + rest <= n_inst - 1)
+
+    def receives(way, hop, rest):
+        return (line(way) >= hop) & (line(way) + rest <= n_inst)
+
+    def hop_target(way, at, hop, rest):
+        source = at - hop
+        if rest == 1:
+            return arrived.at[source if way == 0 else n_inst - 2 - source]
+        return passing.at[way, source * (n_inst - 1 - at) + rest - 2]
+
+    def hop_copy(way, hop, rest):
+        at = line(way)
+        if hop == 1:
+            target = at + rest
+            source = outgoing.at[target - 1 if way == 0 else n_inst - 1 - target]
+        else:
+            source = passing.at[way, (at - hop + 1) * (n_inst - 1 - at) + rest - 1]
+        return pltpu.make_async_remote_copy(
+            src_ref=source,
+            dst_ref=hop_target(way, at + 1, hop, rest),
+            send_sem=hop_send.at[way, hop - 1, rest - 1],
+            recv_sem=hop_recv.at[way, hop - 1, rest - 1],
+            device_id={"inst": inst + 1 - 2 * way, "mp": mp},
+            device_id_type=MESH,
+        )
+
+    def hop_wait(way, hop, rest):
+        @pl.when(receives(way, hop, rest))
+        def _():
+            target = hop_target(way, line(way), hop, rest)
+            pltpu.make_async_remote_copy(
+                src_ref=outgoing.at[0],
+                dst_ref=target,
+                send_sem=hop_send.at[way, hop - 1, rest - 1],
+                recv_sem=hop_recv.at[way, hop - 1, rest - 1],
+                device_id={"inst": inst + 1 - 2 * way, "mp": mp},
+                device_id_type=MESH,
+            ).wait_recv()
+
+    def hop_start(hop):
+        for rest in range(n_inst - hop, 0, -1):
+            for way in range(2):
+                if hop > 1:
+                    hop_wait(way, hop - 1, rest + 1)
+
+                @pl.when(sends(way, hop, rest))
+                def _():
+                    hop_copy(way, hop, rest).start()
 
     def part_copy(j, k):
         to = lax.rem(mp + 1 + k, n_mp)
@@ -198,14 +258,20 @@
             device_id_type=MESH,
         )
 
-    own_copy = pltpu.make_async_copy(
-        stage.at[:, :, columns(own_head)], cache.at[pl.ds(0, requests), mp], own_sem
-    )
-    own_copy.start()
-
-    pl.semaphore_wait(barrier, n_inst * n_mp - 1)
+    own_copies = [
+        pltpu.make_async_copy(
+            stage.at[:, :, columns(own_head)], cache.at[pl.ds(0, requests), mp], own_sem.at[0]
+        ),
+        pltpu.make_async_copy(
+            leaving.at[:, :, columns(own_head)], outgoing.at[:, mp], own_sem.at[1]
+        ),
+    ]
+    for copy in own_copies:
+        copy.start()
+
+    pl.semaphore_wait(barrier, greetings)
+    loop(n_mp - 1, lambda k: leave_copy(k).start())
     loop(n_mp - 1, lambda k: page_copy(k).start())
-    loop(n_inst - 1, lambda k: loop(n_mp, lambda to: mig_copy(k, to, mp).start()))
 
     loads[1].wait()
     features = hidden_v[...].astype(F32).reshape(rows, hidden.shape[2]).astype(BF16)
@@ -224,14 +290,18 @@
 
         loop(n_mp - 1, send_part)
 
-    block = [jnp.int32(r) for r in range(requests)]
+    count = jnp.int32(0)
+    place = [jnp.int32(0)] * migrants
+    guest = [jnp.int32(-1)] * migrants
     for k in range(n_inst - 1):
-        source = lax.rem(inst + 2 * n_inst - 1 - k, n_inst)
-        place = jnp.int32(-1)
+        source = jnp.where(k < inst, k, k + 1)
         for u in range(migrants):
-            place = jnp.where(mig_dest[u, source] == inst, mig_local[u, source], place)
-        for r in range(requests):
-            block[r] = jnp.where(place == r, requests + k, block[r])
+            here = mig_dest[u, source] == inst
+            for v in range(migrants):
+                hit = here & (count == v)
+                place[v] = jnp.where(hit, k, place[v])
+                guest[v] = jnp.where(hit, mig_local[u, source], guest[v])
+            count = count + jnp.where(here, 1, 0)
 
     row8 = lax.broadcasted_iota(jnp.int32, (requests, head_dim), 0)
     length8 = jnp.zeros((requests, head_dim), jnp.int32)
@@ -242,22 +312,40 @@
     lane = lax.broadcasted_iota(jnp.int32, (rows, head_dim), 1)
     pair_index = jnp.where(lane < half, lane, lane - half)
     frequency = jnp.exp(-(2.0 * pair_index.astype(F32) / head_dim) * math.log(1000000.0))
-    place = jnp.concatenate([(length8 + t).astype(F32) for t in range(steps)], axis=0)
-    angle = place * frequency
+    position = jnp.concatenate([(length8 + t).astype(F32) for t in range(steps)], axis=0)
+    angle = position * frequency
     cosine = jnp.cos(angle)
     sine = jnp.sin(angle)
     sine = jnp.where(lane < half, -sine, sine)
 
+    stay8 = length8
+    for v in range(migrants):
+        stay8 = jnp.where(row8 == guest[v], 0, stay8)
     cached_lane = lax.broadcasted_iota(jnp.int32, (requests, requests * context), 1)
     first = lax.broadcasted_iota(jnp.int32, (requests, requests * context), 0) * context
-    last = first + jnp.broadcast_to(length8[:, :1], first.shape)
+    last = first + jnp.broadcast_to(stay8[:, :1], first.shape)
     bias = jnp.where((cached_lane >= first) & (cached_lane < last), 0.0, -1e30).astype(F32)
 
+    guests = migrants * context
+    guest_lane = lax.broadcasted_iota(jnp.int32, (requests, guests), 1)
+    guest_row = lax.broadcasted_iota(jnp.int32, (requests, guests), 0)
+    guest_length = jnp.broadcast_to(length8[:, :1], guest_lane.shape)
+    known = guest_row < 0
+    for v in range(migrants):
+        known = known | (
+            (guest_row == guest[v])
+            & (guest_lane >= v * context)
+            & (guest_lane < v * context + guest_length)
+        )
+    guest_bias = jnp.where(known, 0.0, -1e30).astype(F32)
     row = lax.broadcasted_iota(jnp.int32, (rows, 128), 0)
     column = lax.broadcasted_iota(jnp.int32, (rows, 128), 1)
     fresh_bias = jnp.where(
         (lax.rem(row, requests) == lax.rem(column, requests)) & (column <= row), 0.0, -1e30
     ).astype(F32)
+    late_bias = jnp.concatenate(
+        [jnp.concatenate([guest_bias] * steps, axis=0), fresh_bias], axis=1
+    )
 
     loads[2].wait()
     query = jnp.concatenate(
@@ -268,23 +356,25 @@
         ],
         axis=0,
     ).astype(BF16)
-    value_all[:, head_dim:] = jnp.ones((requests * context, head_dim), BF16)
     scale = 1.0 / math.sqrt(head_dim)
 
-    own_copy.wait()
+    def with_ones(values):
+        return jnp.concatenate([values, jnp.ones(values.shape, BF16)], axis=1)
+
+    own_copies[1].wait()
+    loop(n_mp - 1, lambda k: leave_copy(k).wait_recv())
+    for hop in range(1, n_inst):
+        hop_start(hop)
+
+    own_copies[0].wait()
     loop(n_mp - 1, lambda k: page_copy(k).wait_recv())
-    loop(n_inst - 1, lambda k: loop(n_mp, lambda to: mig_copy(k, to, to).wait_recv()))
-    for r in range(requests):
-        held = cache[block[r]].reshape(context, pair)
-        key_all[r * context : (r + 1) * context, :] = held[:, :head_dim]
-        value_all[r * context : (r + 1) * context, :head_dim] = held[:, head_dim:]
-
+    held = cache[...].reshape(requests * context, pair)
     total_rows = portion * rows
-    scores = dot(query, key_all[...], ((1,), (1,))) * scale
+    scores = dot(query, held[:, :head_dim], ((1,), (1,))) * scale
     scores = scores.reshape(portion * steps, requests, requests * context) + bias[None]
     scores = scores.reshape(total_rows, requests * context)
     peak = jnp.max(scores, axis=-1, keepdims=True)
-    summed = weighted(jnp.exp(scores - peak), value_all[...])
+    summed = weighted(jnp.exp(scores - peak), with_ones(held[:, head_dim:]))
 
     loads[3].wait()
     loop(n_mp - 1, lambda k: part_copy(0, k).wait_recv())
@@ -298,13 +388,21 @@
     blank = jnp.zeros((128 - rows, head_dim), F32)
     fresh_keys = jnp.concatenate([keys, blank], axis=0).astype(BF16)
     fresh_values = jnp.concatenate([projected[:, head_dim:], blank], axis=0).astype(BF16)
-    fresh_values = jnp.concatenate(
-        [fresh_values, jnp.ones((128, head_dim), BF16)], axis=1
-    )
-    fresh = dot(query, fresh_keys, ((1,), (1,))) * scale
-    fresh = (fresh.reshape(portion, rows, 128) + fresh_bias[None]).reshape(total_rows, 128)
-    highest = jnp.maximum(peak, jnp.max(fresh, axis=-1, keepdims=True))
-    summed = summed * jnp.exp(peak - highest) + weighted(jnp.exp(fresh - highest), fresh_values)
+
+    for hop in range(1, n_inst):
+        for way in range(2):
+            hop_wait(way, hop, 1)
+    came = [arrived[place[v]].reshape(context, pair) for v in range(migrants)]
+    late_keys = jnp.concatenate([page[:, :head_dim] for page in came] + [fresh_keys], axis=0)
+    late_values = jnp.concatenate([page[:, head_dim:] for page in came] + [fresh_values], axis=0)
+    late = dot(query, late_keys, ((1,), (1,))) * scale
+    late = (late.reshape(portion, rows, guests + 128) + late_bias[None]).reshape(
+        total_rows, guests + 128
+    )
+    highest = jnp.maximum(peak, jnp.max(late, axis=-1, keepdims=True))
+    summed = summed * jnp.exp(peak - highest) + weighted(
+        jnp.exp(late - highest), with_ones(late_values)
+    )
     result = summed[:, :head_dim] / summed[:, head_dim:]
     for t in range(steps):
         for g in range(portion):
@@ -312,7 +410,15 @@
             out[t, :, g * head_dim : (g + 1) * head_dim] = result[at : at + requests].astype(BF16)
 
     loop(n_mp - 1, lambda k: page_copy(k).wait_send())
-    loop(n_inst - 1, lambda k: loop(n_mp, lambda to: mig_copy(k, to, mp).wait_send()))
+    loop(n_mp - 1, lambda k: leave_copy(k).wait_send())
+    for hop in range(1, n_inst):
+        for rest in range(n_inst - hop, 0, -1):
+            for way in range(2):
+
+                @pl.when(sends(way, hop, rest))
+                def _():
+                    hop_copy(way, hop, rest).wait_send()
+
     loop(n_mp - 1, lambda k: part_copy(0, k).wait_send())
 
 
@@ -340,7 +446,6 @@
     pool = kv_pool[0]
     page = pool.shape[1]
     rows = steps * requests
-    context = n_mp * page
     assert page_table.shape[1] == 1 and n_mp % kv_heads == 0
     far = pl.BlockSpec(memory_space=pltpu.HBM)
     return pl.pallas_call(
@@ -356,11 +461,12 @@
             pltpu.VMEM((steps, requests, portion), BF16),
             pltpu.VMEM((requests, page, width), BF16),
             pltpu.VMEM((n_inst - 1, page, width), BF16),
-            pltpu.VMEM((requests + n_inst - 1, n_mp, page, pair), BF16),
+            pltpu.VMEM((requests, n_mp, page, pair), BF16),
+            pltpu.VMEM((n_inst - 1, n_mp, page, pair), BF16),
+            pltpu.VMEM((2, max(n_inst * n_inst // 4, 1), n_mp, page, pair), BF16),
+            pltpu.VMEM((n_inst - 1, n_mp, page, pair), BF16),
             pltpu.VMEM((kv_heads, rows, pair), F32),
             pltpu.VMEM((n_mp - 1, rows, pair), F32),
-            pltpu.VMEM((requests * context, head_dim), BF16),
-            pltpu.VMEM((requests * context, pair), BF16),
             pltpu.SMEM((requests,), jnp.int32),
             pltpu.SMEM((requests,), jnp.int32),
             pltpu.SMEM((migrants, n_inst), jnp.int32),
@@ -369,11 +475,13 @@
             pltpu.SemaphoreType.DMA((5,)),
             pltpu.SemaphoreType.DMA((4,)),
             pltpu.SemaphoreType.DMA((kv_heads,)),
-            pltpu.SemaphoreType.DMA,
+            pltpu.SemaphoreType.DMA((2,)),
             pltpu.SemaphoreType.DMA((n_mp - 1,)),
             pltpu.SemaphoreType.DMA((n_mp - 1,)),
-            pltpu.SemaphoreType.DMA((n_inst - 1, n_mp)),
-            pltpu.SemaphoreType.DMA((n_inst - 1, n_mp)),
+            pltpu.SemaphoreType.DMA((n_mp - 1,)),
+            pltpu.SemaphoreType.DMA((n_mp - 1,)),
+            pltpu.SemaphoreType.DMA((2, n_inst - 1, n_inst - 1)),
+            pltpu.SemaphoreType.DMA((2, n_inst - 1, n_inst - 1)),
             pltpu.SemaphoreType.DMA((n_mp - 1,)),
             pltpu.SemaphoreType.DMA((n_mp - 1,)),
         ],

time: 14 us -> 18.7 us (1.34)
  Pallas kernels: 13.2 us -> 17.9 us
    pallas_call x1, Pallas kernels: 13.2 us -> 17.9 us  [local(): pl.pallas_call(functools.partial(kernel, n_inst, n_mp, migrants, kv_heads...]
where the time goes in v5:
time: 18.7 us; the launch traced here: 18.5 us
  Pallas kernels  17.9 us (96%)
  local copies, waits for them, and re-layouts  0.62 us (3%)
    pallas_call x1, Pallas kernels, local(): pl.pallas_call(functools.partial(kernel, n_inst, n_mp, migrants, kv_heads...  17.9 us
    unnamed x1, local copies, waits for them, and re-layouts  0.62 us

profile of v5, /device:TPU:0, one launch (start us, length us, event | category | flops | bytes accessed | tf_op | source)
XLA Modules:
  0.0 18.5 jit_solution(6377386965921280035)
XLA Ops:
  0.0 17.9 %shard_map.100 = bf16[3,8,1024]{2,1,0:T(8,128)(2,1)S(1)} custom-call(s32[8]{0:T(128)} %bitcast.9, s32[8]{0:T(128)} %length_h.1, s32[2,4]{1,0:T(2,128)} %bitcast.7, s32[2,4]{1,0:T(2,128)} %bitcast.8, s32[2]{0:T(128)} %bitcast.10, bf16[3,8,1280]{2,1,0:T(8,128)(2,1)} %hidden.1, bf16[1280,1024]{1,0:T(8,128)(2,1)} %weight.1, f32[1,128]{1,0:T(1,128)} %bitcast.11, ...), custom_call_target="tpu_custom_call" | custom-call | tf_op jit(solution)/shard_map/pallas_call | solution.py:451
  17.9 0.6 %copy.12 = bf16[3,8,1024]{2,1,0:T(8,128)(2,1)} copy(bf16[3,8,1024]{2,1,0:T(8,128)(2,1)S(1)} %shard_map.100) | data formatting | bytes 98304

commit v6 on v5

--- a/solution.py
+++ b/solution.py
@@ -56,7 +56,7 @@
     leaving,
     cache,
     outgoing,
-    passing,
+    moving,
     arrived,
     part_out,
     part_in,
@@ -73,8 +73,9 @@
     page_recv,
     leave_send,
     leave_recv,
-    hop_send,
-    hop_recv,
+    move_send,
+    move_recv,
+    news,
     part_send,
     part_recv,
 ):
@@ -128,10 +129,10 @@
     for load in int_loads:
         load.start()
     loads[1].start()
+    loads[2].start()
+    loads[3].start()
     for load in weight_loads:
         load.start()
-    loads[2].start()
-    loads[3].start()
 
     barrier = pltpu.get_barrier_semaphore()
 
@@ -162,14 +163,8 @@
     for r in range(requests):
         stage[r] = pool_v[table[r]]
 
-    def take_leaving(k):
-        to_inst = jnp.where(k < inst, k, k + 1)
-        slot = mig_slot[0]
-        for u in range(1, migrants):
-            slot = jnp.where(mig_dest[u, inst] == to_inst, mig_slot[u], slot)
-        leaving[k] = pool_v[slot]
-
-    loop(n_inst - 1, take_leaving)
+    for u in range(migrants):
+        leaving[u] = pool_v[mig_slot[u]]
 
     def page_copy(k):
         to = lax.rem(mp + 1 + k, n_mp)
@@ -193,59 +188,50 @@
             device_id_type=MESH,
         )
 
+    def move_copy(k):
+        to = jnp.where(k < inst, k, k + 1)
+        return pltpu.make_async_remote_copy(
+            src_ref=moving.at[k],
+            dst_ref=arrived.at[jnp.where(inst < to, inst, inst - 1)],
+            send_sem=move_send.at[k],
+            recv_sem=move_recv.at[jnp.where(inst < to, inst, inst - 1)],
+            device_id={"inst": to, "mp": mp},
+            device_id_type=MESH,
+        )
+
+    def move_wait(k):
+        source = jnp.where(k < inst, k, k + 1)
+        pltpu.make_async_remote_copy(
+            src_ref=moving.at[k],
+            dst_ref=arrived.at[k],
+            send_sem=move_send.at[k],
+            recv_sem=move_recv.at[k],
+            device_id={"inst": source, "mp": mp},
+            device_id_type=MESH,
+        ).wait_recv()
+
     def line(way):
         return inst if way == 0 else n_inst - 1 - inst
 
-    def sends(way, hop, rest):
-        return (line(way) >= hop - 1) & (line(way) + rest <= n_inst - 1)
-
-    def receives(way, hop, rest):
-        return (line(way) >= hop) & (line(way) + rest <= n_inst)
-
-    def hop_target(way, at, hop, rest):
-        source = at - hop
-        if rest == 1:
-            return arrived.at[source if way == 0 else n_inst - 2 - source]
-        return passing.at[way, source * (n_inst - 1 - at) + rest - 2]
-
-    def hop_copy(way, hop, rest):
-        at = line(way)
-        if hop == 1:
-            target = at + rest
-            source = outgoing.at[target - 1 if way == 0 else n_inst - 1 - target]
-        else:
-            source = passing.at[way, (at - hop + 1) * (n_inst - 1 - at) + rest - 1]
-        return pltpu.make_async_remote_copy(
-            src_ref=source,
-            dst_ref=hop_target(way, at + 1, hop, rest),
-            send_sem=hop_send.at[way, hop - 1, rest - 1],
-            recv_sem=hop_recv.at[way, hop - 1, rest - 1],
-            device_id={"inst": inst + 1 - 2 * way, "mp": mp},
-            device_id_type=MESH,
-        )
-
-    def hop_wait(way, hop, rest):
-        @pl.when(receives(way, hop, rest))
+    def tell(way, far):
+        @pl.when((line(way) > 0) & (line(way) + far <= n_inst - 1))
         def _():
-            target = hop_target(way, line(way), hop, rest)
-            pltpu.make_async_remote_copy(
-                src_ref=outgoing.at[0],
-                dst_ref=target,
-                send_sem=hop_send.at[way, hop - 1, rest - 1],
-                recv_sem=hop_recv.at[way, hop - 1, rest - 1],
-                device_id={"inst": inst + 1 - 2 * way, "mp": mp},
+            pl.semaphore_signal(
+                news.at[way, far - 1],
+                inc=1,
+                device_id={"inst": inst - 1 + 2 * way, "mp": mp},
                 device_id_type=MESH,
-            ).wait_recv()
-
-    def hop_start(hop):
-        for rest in range(n_inst - hop, 0, -1):
-            for way in range(2):
-                if hop > 1:
-                    hop_wait(way, hop - 1, rest + 1)
-
-                @pl.when(sends(way, hop, rest))
-                def _():
-                    hop_copy(way, hop, rest).start()
+            )
+
+    def hear(far):
+        for way in range(2):
+
+            @pl.when(line(way) + 1 + far <= n_inst - 1)
+            def _():
+                pl.semaphore_wait(news.at[way, far - 1], 1)
+
+            if far + 1 <= n_inst - 2:
+                tell(way, far + 1)
 
     def part_copy(j, k):
         to = lax.rem(mp + 1 + k, n_mp)
@@ -268,27 +254,6 @@
     ]
     for copy in own_copies:
         copy.start()
-
-    pl.semaphore_wait(barrier, greetings)
-    loop(n_mp - 1, lambda k: leave_copy(k).start())
-    loop(n_mp - 1, lambda k: page_copy(k).start())
-
-    loads[1].wait()
-    features = hidden_v[...].astype(F32).reshape(rows, hidden.shape[2]).astype(BF16)
-    for j in range(kv_heads):
-        weight_loads[j].wait()
-        part_out[j] = dot(features, weight_v[j])
-        if share == 1:
-            if j < kv_heads - 1:
-                part_copy(j, j).start()
-    if share > 1:
-
-        def send_part(k):
-            to = lax.rem(mp + 1 + k, n_mp)
-            j = lax.rem(to // share - own_head - 1 + 2 * kv_heads, kv_heads)
-            part_copy(j, k).start()
-
-        loop(n_mp - 1, send_part)
 
     count = jnp.int32(0)
     place = [jnp.int32(0)] * migrants
@@ -356,6 +321,32 @@
         ],
         axis=0,
     ).astype(BF16)
+    pl.semaphore_wait(barrier, greetings)
+    loop(n_mp - 1, lambda k: leave_copy(k).start())
+    loop(n_mp - 1, lambda k: page_copy(k).start())
+    if n_inst > 2:
+        for way in range(2):
+            tell(way, 1)
+
+    loads[1].wait()
+    features = hidden_v[...].astype(F32).reshape(rows, hidden.shape[2]).astype(BF16)
+    for j in range(kv_heads):
+        weight_loads[j].wait()
+        part_out[j] = dot(features, weight_v[j])
+        if share == 1:
+            if j < kv_heads - 1:
+                part_copy(j, j).start()
+        if j == 1 and n_inst > 2:
+            hear(1)
+    if share > 1:
+
+        def send_part(k):
+            to = lax.rem(mp + 1 + k, n_mp)
+            j = lax.rem(to // share - own_head - 1 + 2 * kv_heads, kv_heads)
+            part_copy(j, k).start()
+
+        loop(n_mp - 1, send_part)
+
     scale = 1.0 / math.sqrt(head_dim)
 
     def with_ones(values):
@@ -363,8 +354,18 @@
 
     own_copies[1].wait()
     loop(n_mp - 1, lambda k: leave_copy(k).wait_recv())
-    for hop in range(1, n_inst):
-        hop_start(hop)
+    for far in range(2, n_inst - 1):
+        hear(far)
+
+    def take_moving(k):
+        to = jnp.where(k < inst, k, k + 1)
+        chosen = jnp.int32(0)
+        for u in range(1, migrants):
+            chosen = jnp.where(mig_dest[u, inst] == to, u, chosen)
+        moving[k] = outgoing[chosen]
+        move_copy(k).start()
+
+    loop(n_inst - 1, take_moving)
 
     own_copies[0].wait()
     loop(n_mp - 1, lambda k: page_copy(k).wait_recv())
@@ -389,9 +390,7 @@
     fresh_keys = jnp.concatenate([keys, blank], axis=0).astype(BF16)
     fresh_values = jnp.concatenate([projected[:, head_dim:], blank], axis=0).astype(BF16)
 
-    for hop in range(1, n_inst):
-        for way in range(2):
-            hop_wait(way, hop, 1)
+    loop(n_inst - 1, move_wait)
     came = [arrived[place[v]].reshape(context, pair) for v in range(migrants)]
     late_keys = jnp.concatenate([page[:, :head_dim] for page in came] + [fresh_keys], axis=0)
     late_values = jnp.concatenate([page[:, head_dim:] for page in came] + [fresh_values], axis=0)
@@ -411,14 +410,7 @@
 
     loop(n_mp - 1, lambda k: page_copy(k).wait_send())
     loop(n_mp - 1, lambda k: leave_copy(k).wait_send())
-    for hop in range(1, n_inst):
-        for rest in range(n_inst - hop, 0, -1):
-            for way in range(2):
-
-                @pl.when(sends(way, hop, rest))
-                def _():
-                    hop_copy(way, hop, rest).wait_send()
-
+    loop(n_inst - 1, lambda k: move_copy(k).wait_send())
     loop(n_mp - 1, lambda k: part_copy(0, k).wait_send())
 
 
@@ -460,10 +452,10 @@
             pltpu.VMEM((1, head_dim), F32),
             pltpu.VMEM((steps, requests, portion), BF16),
             pltpu.VMEM((requests, page, width), BF16),
-            pltpu.VMEM((n_inst - 1, page, width), BF16),
+            pltpu.VMEM((migrants, page, width), BF16),
             pltpu.VMEM((requests, n_mp, page, pair), BF16),
+            pltpu.VMEM((migrants, n_mp, page, pair), BF16),
             pltpu.VMEM((n_inst - 1, n_mp, page, pair), BF16),
-            pltpu.VMEM((2, max(n_inst * n_inst // 4, 1), n_mp, page, pair), BF16),
             pltpu.VMEM((n_inst - 1, n_mp, page, pair), BF16),
             pltpu.VMEM((kv_heads, rows, pair), F32),
             pltpu.VMEM((n_mp - 1, rows, pair), F32),
@@ -480,8 +472,9 @@
             pltpu.SemaphoreType.DMA((n_mp - 1,)),
             pltpu.SemaphoreType.DMA((n_mp - 1,)),
             pltpu.SemaphoreType.DMA((n_mp - 1,)),
-            pltpu.SemaphoreType.DMA((2, n_inst - 1, n_inst - 1)),
-            pltpu.SemaphoreType.DMA((2, n_inst - 1, n_inst - 1)),
+            pltpu.SemaphoreType.DMA((n_inst - 1,)),
+            pltpu.SemaphoreType.DMA((n_inst - 1,)),
+            pltpu.SemaphoreType.REGULAR((2, n_inst)),
             pltpu.SemaphoreType.DMA((n_mp - 1,)),
             pltpu.SemaphoreType.DMA((n_mp - 1,)),
         ],

time: 18.7 us -> 14 us (0.75)
  Pallas kernels: 17.9 us -> 13.2 us
    pallas_call x1, Pallas kernels: 17.9 us -> 13.2 us  [local(): pl.pallas_call(functools.partial(kernel, n_inst, n_mp, migrants, kv_heads...]
where the time goes in v6:
time: 14 us; the launch traced here: 13.9 us
  Pallas kernels  13.2 us (94%)
  local copies, waits for them, and re-layouts  0.62 us (4%)
    pallas_call x1, Pallas kernels, local(): pl.pallas_call(functools.partial(kernel, n_inst, n_mp, migrants, kv_heads...  13.2 us
    unnamed x1, local copies, waits for them, and re-layouts  0.62 us

profile of v6, /device:TPU:0, one launch (start us, length us, event | category | flops | bytes accessed | tf_op | source)
XLA Modules:
  0.0 13.9 jit_solution(2628784298115827723)
XLA Ops:
  0.0 13.2 %shard_map.100 = bf16[3,8,1024]{2,1,0:T(8,128)(2,1)S(1)} custom-call(s32[8]{0:T(128)} %bitcast.9, s32[8]{0:T(128)} %length_h.1, s32[2,4]{1,0:T(2,128)} %bitcast.7, s32[2,4]{1,0:T(2,128)} %bitcast.8, s32[2]{0:T(128)} %bitcast.10, bf16[3,8,1280]{2,1,0:T(8,128)(2,1)} %hidden.1, bf16[1280,1024]{1,0:T(8,128)(2,1)} %weight.1, f32[1,128]{1,0:T(1,128)} %bitcast.11, ...), custom_call_target="tpu_custom_call" | custom-call | tf_op jit(solution)/shard_map/pallas_call | solution.py:443
  13.2 0.6 %copy.12 = bf16[3,8,1024]{2,1,0:T(8,128)(2,1)} copy(bf16[3,8,1024]{2,1,0:T(8,128)(2,1)S(1)} %shard_map.100) | data formatting | bytes 98304

commit v7 on v6

--- a/solution.py
+++ b/solution.py
@@ -55,8 +55,6 @@
     stage,
     leaving,
     cache,
-    outgoing,
-    moving,
     arrived,
     part_out,
     part_in,
@@ -71,8 +69,6 @@
     own_sem,
     page_send,
     page_recv,
-    leave_send,
-    leave_recv,
     move_send,
     move_recv,
     news,
@@ -93,6 +89,29 @@
 
     def columns(head):
         return pl.ds(pl.multiple_of(head * pair, pair), pair)
+
+    barrier = pltpu.get_barrier_semaphore()
+
+    def greet_peer(k):
+        pl.semaphore_signal(
+            barrier,
+            inc=1,
+            device_id={"inst": inst, "mp": lax.rem(mp + 1 + k, n_mp)},
+            device_id_type=MESH,
+        )
+
+    loop(n_mp - 1, greet_peer)
+    for away, there in ((1, inst < n_inst - 1), (-1, inst > 0)):
+
+        @pl.when(there)
+        def _():
+            pl.semaphore_signal(
+                barrier, inc=1, device_id={"inst": inst + away, "mp": mp}, device_id_type=MESH
+            )
+
+    greetings = (
+        n_mp - 1 + jnp.where(inst < n_inst - 1, 1, 0) + jnp.where(inst > 0, 1, 0)
+    )
 
     loads = [
         pltpu.make_async_copy(pool, pool_v, in_sem.at[0]),
@@ -134,37 +153,20 @@
     for load in weight_loads:
         load.start()
 
-    barrier = pltpu.get_barrier_semaphore()
-
-    def greet_peer(k):
-        pl.semaphore_signal(
-            barrier,
-            inc=1,
-            device_id={"inst": inst, "mp": lax.rem(mp + 1 + k, n_mp)},
-            device_id_type=MESH,
-        )
-
-    loop(n_mp - 1, greet_peer)
-    for away, there in ((1, inst < n_inst - 1), (-1, inst > 0)):
-
-        @pl.when(there)
-        def _():
-            pl.semaphore_signal(
-                barrier, inc=1, device_id={"inst": inst + away, "mp": mp}, device_id_type=MESH
-            )
-
-    greetings = (
-        n_mp - 1 + jnp.where(inst < n_inst - 1, 1, 0) + jnp.where(inst > 0, 1, 0)
-    )
-
     for load in int_loads:
         load.wait()
     loads[0].wait()
     for r in range(requests):
         stage[r] = pool_v[table[r]]
 
-    for u in range(migrants):
-        leaving[u] = pool_v[mig_slot[u]]
+    def take_leaving(k):
+        to_inst = jnp.where(k < inst, k, k + 1)
+        slot = mig_slot[0]
+        for u in range(1, migrants):
+            slot = jnp.where(mig_dest[u, inst] == to_inst, mig_slot[u], slot)
+        leaving[k] = pool_v[slot]
+
+    loop(n_inst - 1, take_leaving)
 
     def page_copy(k):
         to = lax.rem(mp + 1 + k, n_mp)
@@ -177,36 +179,26 @@
             device_id_type=MESH,
         )
 
-    def leave_copy(k):
-        to = lax.rem(mp + 1 + k, n_mp)
+    def move_copy(way, far, to):
+        target = inst + (1 + far) * (1 - 2 * way)
+        place = target - 1 + way
+        here = inst - way
         return pltpu.make_async_remote_copy(
-            src_ref=leaving.at[:, :, columns(to // share)],
-            dst_ref=outgoing.at[:, mp],
-            send_sem=leave_send.at[k],
-            recv_sem=leave_recv.at[k],
-            device_id={"inst": inst, "mp": to},
+            src_ref=leaving.at[place, :, columns(to // share)],
+            dst_ref=arrived.at[here, mp],
+            send_sem=move_send.at[place, to],
+            recv_sem=move_recv.at[here, mp],
+            device_id={"inst": target, "mp": to},
             device_id_type=MESH,
         )
 
-    def move_copy(k):
-        to = jnp.where(k < inst, k, k + 1)
-        return pltpu.make_async_remote_copy(
-            src_ref=moving.at[k],
-            dst_ref=arrived.at[jnp.where(inst < to, inst, inst - 1)],
-            send_sem=move_send.at[k],
-            recv_sem=move_recv.at[jnp.where(inst < to, inst, inst - 1)],
-            device_id={"inst": to, "mp": mp},
-            device_id_type=MESH,
-        )
-
-    def move_wait(k):
-        source = jnp.where(k < inst, k, k + 1)
+    def move_wait(k, column):
         pltpu.make_async_remote_copy(
-            src_ref=moving.at[k],
-            dst_ref=arrived.at[k],
-            send_sem=move_send.at[k],
-            recv_sem=move_recv.at[k],
-            device_id={"inst": source, "mp": mp},
+            src_ref=leaving.at[k, :, columns(0)],
+            dst_ref=arrived.at[k, column],
+            send_sem=move_send.at[k, column],
+            recv_sem=move_recv.at[k, column],
+            device_id={"inst": jnp.where(k < inst, k, k + 1), "mp": column},
             device_id_type=MESH,
         ).wait_recv()
 
@@ -217,7 +209,7 @@
         @pl.when((line(way) > 0) & (line(way) + far <= n_inst - 1))
         def _():
             pl.semaphore_signal(
-                news.at[way, far - 1],
+                news.at[way, far],
                 inc=1,
                 device_id={"inst": inst - 1 + 2 * way, "mp": mp},
                 device_id_type=MESH,
@@ -228,10 +220,14 @@
 
             @pl.when(line(way) + 1 + far <= n_inst - 1)
             def _():
-                pl.semaphore_wait(news.at[way, far - 1], 1)
+                pl.semaphore_wait(news.at[way, far], 1)
 
             if far + 1 <= n_inst - 2:
                 tell(way, far + 1)
+
+            @pl.when(line(way) + 1 + far <= n_inst - 1)
+            def _():
+                loop(n_mp, lambda to: move_copy(way, far, to).start())
 
     def part_copy(j, k):
         to = lax.rem(mp + 1 + k, n_mp)
@@ -247,9 +243,6 @@
     own_copies = [
         pltpu.make_async_copy(
             stage.at[:, :, columns(own_head)], cache.at[pl.ds(0, requests), mp], own_sem.at[0]
-        ),
-        pltpu.make_async_copy(
-            leaving.at[:, :, columns(own_head)], outgoing.at[:, mp], own_sem.at[1]
         ),
     ]
     for copy in own_copies:
@@ -322,11 +315,9 @@
         axis=0,
     ).astype(BF16)
     pl.semaphore_wait(barrier, greetings)
-    loop(n_mp - 1, lambda k: leave_copy(k).start())
     loop(n_mp - 1, lambda k: page_copy(k).start())
-    if n_inst > 2:
-        for way in range(2):
-            tell(way, 1)
+    for way in range(2):
+        tell(way, 0)
 
     loads[1].wait()
     features = hidden_v[...].astype(F32).reshape(rows, hidden.shape[2]).astype(BF16)
@@ -336,8 +327,8 @@
         if share == 1:
             if j < kv_heads - 1:
                 part_copy(j, j).start()
-        if j == 1 and n_inst > 2:
-            hear(1)
+        if j % 2 == 1 and j // 2 < n_inst - 1:
+            hear(j // 2)
     if share > 1:
 
         def send_part(k):
@@ -352,20 +343,8 @@
     def with_ones(values):
         return jnp.concatenate([values, jnp.ones(values.shape, BF16)], axis=1)
 
-    own_copies[1].wait()
-    loop(n_mp - 1, lambda k: leave_copy(k).wait_recv())
-    for far in range(2, n_inst - 1):
+    for far in range(min(kv_heads // 2, n_inst - 1), n_inst - 1):
         hear(far)
-
-    def take_moving(k):
-        to = jnp.where(k < inst, k, k + 1)
-        chosen = jnp.int32(0)
-        for u in range(1, migrants):
-            chosen = jnp.where(mig_dest[u, inst] == to, u, chosen)
-        moving[k] = outgoing[chosen]
-        move_copy(k).start()
-
-    loop(n_inst - 1, take_moving)
 
     own_copies[0].wait()
     loop(n_mp - 1, lambda k: page_copy(k).wait_recv())
@@ -390,7 +369,7 @@
     fresh_keys = jnp.concatenate([keys, blank], axis=0).astype(BF16)
     fresh_values = jnp.concatenate([projected[:, head_dim:], blank], axis=0).astype(BF16)
 
-    loop(n_inst - 1, move_wait)
+    loop(n_inst - 1, lambda k: loop(n_mp, lambda column: move_wait(k, column)))
     came = [arrived[place[v]].reshape(context, pair) for v in range(migrants)]
     late_keys = jnp.concatenate([page[:, :head_dim] for page in came] + [fresh_keys], axis=0)
     late_values = jnp.concatenate([page[:, head_dim:] for page in came] + [fresh_values], axis=0)
@@ -409,8 +388,13 @@
             out[t, :, g * head_dim : (g + 1) * head_dim] = result[at : at + requests].astype(BF16)
 
     loop(n_mp - 1, lambda k: page_copy(k).wait_send())
-    loop(n_mp - 1, lambda k: leave_copy(k).wait_send())
-    loop(n_inst - 1, lambda k: move_copy(k).wait_send())
+    for far in range(n_inst - 1):
+        for way in range(2):
+
+            @pl.when(line(way) + 1 + far <= n_inst - 1)
+            def _():
+                loop(n_mp, lambda to: move_copy(way, far, to).wait_send())
+
     loop(n_mp - 1, lambda k: part_copy(0, k).wait_send())
 
 
@@ -452,10 +436,8 @@
             pltpu.VMEM((1, head_dim), F32),
             pltpu.VMEM((steps, requests, portion), BF16),
             pltpu.VMEM((requests, page, width), BF16),
-            pltpu.VMEM((migrants, page, width), BF16),
+            pltpu.VMEM((n_inst - 1, page, width), BF16),
             pltpu.VMEM((requests, n_mp, page, pair), BF16),
-            pltpu.VMEM((migrants, n_mp, page, pair), BF16),
-            pltpu.VMEM((n_inst - 1, n_mp, page, pair), BF16),
             pltpu.VMEM((n_inst - 1, n_mp, page, pair), BF16),
             pltpu.VMEM((kv_heads, rows, pair), F32),
             pltpu.VMEM((n_mp - 1, rows, pair), F32),
@@ -470,10 +452,8 @@
             pltpu.SemaphoreType.DMA((2,)),
             pltpu.SemaphoreType.DMA((n_mp - 1,)),
             pltpu.SemaphoreType.DMA((n_mp - 1,)),
-            pltpu.SemaphoreType.DMA((n_mp - 1,)),
-            pltpu.SemaphoreType.DMA((n_mp - 1,)),
-            pltpu.SemaphoreType.DMA((n_inst - 1,)),
-            pltpu.SemaphoreType.DMA((n_inst - 1,)),
+            pltpu.SemaphoreType.DMA((n_inst - 1, n_mp)),
+            pltpu.SemaphoreType.DMA((n_inst - 1, n_mp)),
             pltpu.SemaphoreType.REGULAR((2, n_inst)),
             pltpu.SemaphoreType.DMA((n_mp - 1,)),
             pltpu.SemaphoreType.DMA((n_mp - 1,)),

time: 14 us -> 13.5 us (0.964)
  Pallas kernels: 13.2 us -> 12.7 us
    pallas_call x1, Pallas kernels: 13.2 us -> 12.7 us  [local(): pl.pallas_call(functools.partial(kernel, n_inst, n_mp, migrants, kv_heads...]
where the time goes in v7:
time: 13.5 us; the launch traced here: 13.3 us
  Pallas kernels  12.7 us (94%)
  local copies, waits for them, and re-layouts  0.62 us (5%)
    pallas_call x1, Pallas kernels, local(): pl.pallas_call(functools.partial(kernel, n_inst, n_mp, migrants, kv_heads...  12.7 us
    unnamed x1, local copies, waits for them, and re-layouts  0.62 us

profile of v7, /device:TPU:0, one launch (start us, length us, event | category | flops | bytes accessed | tf_op | source)
XLA Modules:
  0.0 13.3 jit_solution(622846432564982231)
XLA Ops:
  0.0 12.7 %shard_map.100 = bf16[3,8,1024]{2,1,0:T(8,128)(2,1)S(1)} custom-call(s32[8]{0:T(128)} %bitcast.9, s32[8]{0:T(128)} %length_h.1, s32[2,4]{1,0:T(2,128)} %bitcast.7, s32[2,4]{1,0:T(2,128)} %bitcast.8, s32[2]{0:T(128)} %bitcast.10, bf16[3,8,1280]{2,1,0:T(8,128)(2,1)} %hidden.1, bf16[1280,1024]{1,0:T(8,128)(2,1)} %weight.1, f32[1,128]{1,0:T(1,128)} %bitcast.11, ...), custom_call_target="tpu_custom_call" | custom-call | tf_op jit(solution)/shard_map/pallas_call | solution.py:427
  12.7 0.6 %copy.12 = bf16[3,8,1024]{2,1,0:T(8,128)(2,1)} copy(bf16[3,8,1024]{2,1,0:T(8,128)(2,1)S(1)} %shard_map.100) | data formatting | bytes 98304

commit v8 on v7

--- a/solution.py
+++ b/solution.py
@@ -301,10 +301,6 @@
     fresh_bias = jnp.where(
         (lax.rem(row, requests) == lax.rem(column, requests)) & (column <= row), 0.0, -1e30
     ).astype(F32)
-    late_bias = jnp.concatenate(
-        [jnp.concatenate([guest_bias] * steps, axis=0), fresh_bias], axis=1
-    )
-
     loads[2].wait()
     query = jnp.concatenate(
         [
@@ -327,8 +323,8 @@
         if share == 1:
             if j < kv_heads - 1:
                 part_copy(j, j).start()
-        if j % 2 == 1 and j // 2 < n_inst - 1:
-            hear(j // 2)
+        if j < n_inst - 1:
+            hear(j)
     if share > 1:
 
         def send_part(k):
@@ -343,7 +339,7 @@
     def with_ones(values):
         return jnp.concatenate([values, jnp.ones(values.shape, BF16)], axis=1)
 
-    for far in range(min(kv_heads // 2, n_inst - 1), n_inst - 1):
+    for far in range(min(kv_heads, n_inst - 1), n_inst - 1):
         hear(far)
 
     own_copies[0].wait()
@@ -369,17 +365,24 @@
     fresh_keys = jnp.concatenate([keys, blank], axis=0).astype(BF16)
     fresh_values = jnp.concatenate([projected[:, head_dim:], blank], axis=0).astype(BF16)
 
+    fresh = dot(query, fresh_keys, ((1,), (1,))) * scale
+    fresh = (fresh.reshape(portion, rows, 128) + fresh_bias[None]).reshape(total_rows, 128)
+    highest = jnp.maximum(peak, jnp.max(fresh, axis=-1, keepdims=True))
+    summed = summed * jnp.exp(peak - highest) + weighted(
+        jnp.exp(fresh - highest), with_ones(fresh_values)
+    )
+
     loop(n_inst - 1, lambda k: loop(n_mp, lambda column: move_wait(k, column)))
-    came = [arrived[place[v]].reshape(context, pair) for v in range(migrants)]
-    late_keys = jnp.concatenate([page[:, :head_dim] for page in came] + [fresh_keys], axis=0)
-    late_values = jnp.concatenate([page[:, head_dim:] for page in came] + [fresh_values], axis=0)
-    late = dot(query, late_keys, ((1,), (1,))) * scale
-    late = (late.reshape(portion, rows, guests + 128) + late_bias[None]).reshape(
-        total_rows, guests + 128
-    )
+    came = jnp.concatenate(
+        [arrived[place[v]].reshape(context, pair) for v in range(migrants)], axis=0
+    )
+    late = dot(query, came[:, :head_dim], ((1,), (1,))) * scale
+    late = late.reshape(portion * steps, requests, guests) + guest_bias[None]
+    late = late.reshape(total_rows, guests)
+    peak = highest
     highest = jnp.maximum(peak, jnp.max(late, axis=-1, keepdims=True))
     summed = summed * jnp.exp(peak - highest) + weighted(
-        jnp.exp(late - highest), with_ones(late_values)
+        jnp.exp(late - highest), with_ones(came[:, head_dim:])
     )
     result = summed[:, :head_dim] / summed[:, head_dim:]
     for t in range(steps):

time: 13.5 us -> 13.5 us (level)
  no operation moved by 1% of the time
where the time goes in v8:
time: 13.5 us; the launch traced here: 13.3 us
  Pallas kernels  12.7 us (94%)
  local copies, waits for them, and re-layouts  0.62 us (5%)
    pallas_call x1, Pallas kernels, local(): pl.pallas_call(functools.partial(kernel, n_inst, n_mp, migrants, kv_heads...  12.7 us
    unnamed x1, local copies, waits for them, and re-layouts  0.62 us

profile of v8, /device:TPU:0, one launch (start us, length us, event | category | flops | bytes accessed | tf_op | source)
XLA Modules:
  0.0 13.3 jit_solution(2148463956530712661)
XLA Ops:
  0.0 12.7 %shard_map.100 = bf16[3,8,1024]{2,1,0:T(8,128)(2,1)S(1)} custom-call(s32[8]{0:T(128)} %bitcast.9, s32[8]{0:T(128)} %length_h.1, s32[2,4]{1,0:T(2,128)} %bitcast.7, s32[2,4]{1,0:T(2,128)} %bitcast.8, s32[2]{0:T(128)} %bitcast.10, bf16[3,8,1280]{2,1,0:T(8,128)(2,1)} %hidden.1, bf16[1280,1024]{1,0:T(8,128)(2,1)} %weight.1, f32[1,128]{1,0:T(1,128)} %bitcast.11, ...), custom_call_target="tpu_custom_call" | custom-call | tf_op jit(solution)/shard_map/pallas_call | solution.py:430
  12.7 0.6 %copy.12 = bf16[3,8,1024]{2,1,0:T(8,128)(2,1)} copy(bf16[3,8,1024]{2,1,0:T(8,128)(2,1)S(1)} %shard_map.100) | data formatting | bytes 98304

commit v9 on v8

--- a/solution.py
+++ b/solution.py
@@ -215,8 +215,8 @@
                 device_id_type=MESH,
             )
 
-    def hear(far):
-        for way in range(2):
+    def hear(far, ways):
+        for way in ways:
 
             @pl.when(line(way) + 1 + far <= n_inst - 1)
             def _():
@@ -311,9 +311,11 @@
         axis=0,
     ).astype(BF16)
     pl.semaphore_wait(barrier, greetings)
-    loop(n_mp - 1, lambda k: page_copy(k).start())
     for way in range(2):
         tell(way, 0)
+    loop(n_mp - 1, lambda k: page_copy(k).start())
+    for far in range(n_inst - 1):
+        hear(far, (1,))
 
     loads[1].wait()
     features = hidden_v[...].astype(F32).reshape(rows, hidden.shape[2]).astype(BF16)
@@ -324,7 +326,7 @@
             if j < kv_heads - 1:
                 part_copy(j, j).start()
         if j < n_inst - 1:
-            hear(j)
+            hear(j, (0,))
     if share > 1:
 
         def send_part(k):
@@ -340,7 +342,7 @@
         return jnp.concatenate([values, jnp.ones(values.shape, BF16)], axis=1)
 
     for far in range(min(kv_heads, n_inst - 1), n_inst - 1):
-        hear(far)
+        hear(far, (0,))
 
     own_copies[0].wait()
     loop(n_mp - 1, lambda k: page_copy(k).wait_recv())

time: 13.5 us -> 12.3 us (0.911)
  Pallas kernels: 12.7 us -> 11.5 us
    pallas_call x1, Pallas kernels: 12.7 us -> 11.5 us  [local(): pl.pallas_call(functools.partial(kernel, n_inst, n_mp, migrants, kv_heads...]
where the time goes in v9:
time: 12.3 us; the launch traced here: 12.2 us
  Pallas kernels  11.5 us (93%)
  local copies, waits for them, and re-layouts  0.62 us (5%)
    pallas_call x1, Pallas kernels, local(): pl.pallas_call(functools.partial(kernel, n_inst, n_mp, migrants, kv_heads...  11.5 us
    unnamed x1, local copies, waits for them, and re-layouts  0.62 us

profile of v9, /device:TPU:0, one launch (start us, length us, event | category | flops | bytes accessed | tf_op | source)
XLA Modules:
  0.0 12.2 jit_solution(13193894635679391585)
XLA Ops:
  0.0 11.5 %shard_map.100 = bf16[3,8,1024]{2,1,0:T(8,128)(2,1)S(1)} custom-call(s32[8]{0:T(128)} %bitcast.9, s32[8]{0:T(128)} %length_h.1, s32[2,4]{1,0:T(2,128)} %bitcast.7, s32[2,4]{1,0:T(2,128)} %bitcast.8, s32[2]{0:T(128)} %bitcast.10, bf16[3,8,1280]{2,1,0:T(8,128)(2,1)} %hidden.1, bf16[1280,1024]{1,0:T(8,128)(2,1)} %weight.1, f32[1,128]{1,0:T(1,128)} %bitcast.11, ...), custom_call_target="tpu_custom_call" | custom-call | tf_op jit(solution)/shard_map/pallas_call | solution.py:432
  11.6 0.6 %copy.12 = bf16[3,8,1024]{2,1,0:T(8,128)(2,1)} copy(bf16[3,8,1024]{2,1,0:T(8,128)(2,1)S(1)} %shard_map.100) | data formatting | bytes 98304

commit v10 on v9

--- a/solution.py
+++ b/solution.py
@@ -313,9 +313,9 @@
     pl.semaphore_wait(barrier, greetings)
     for way in range(2):
         tell(way, 0)
-    loop(n_mp - 1, lambda k: page_copy(k).start())
     for far in range(n_inst - 1):
         hear(far, (1,))
+    loop(n_mp - 1, lambda k: page_copy(k).start())
 
     loads[1].wait()
     features = hidden_v[...].astype(F32).reshape(rows, hidden.shape[2]).astype(BF16)

time: 12.3 us -> 12.3 us (level)
  no operation moved by 1% of the time
where the time goes in v10:
time: 12.3 us; the launch traced here: 12.2 us
  Pallas kernels  11.5 us (93%)
  local copies, waits for them, and re-layouts  0.62 us (5%)
    pallas_call x1, Pallas kernels, local(): pl.pallas_call(functools.partial(kernel, n_inst, n_mp, migrants, kv_heads...  11.5 us
    unnamed x1, local copies, waits for them, and re-layouts  0.62 us

profile of v10, /device:TPU:0, one launch (start us, length us, event | category | flops | bytes accessed | tf_op | source)
XLA Modules:
  0.0 12.2 jit_solution(115528851633885518)
XLA Ops:
  0.0 11.5 %shard_map.100 = bf16[3,8,1024]{2,1,0:T(8,128)(2,1)S(1)} custom-call(s32[8]{0:T(128)} %bitcast.9, s32[8]{0:T(128)} %length_h.1, s32[2,4]{1,0:T(2,128)} %bitcast.7, s32[2,4]{1,0:T(2,128)} %bitcast.8, s32[2]{0:T(128)} %bitcast.10, bf16[3,8,1280]{2,1,0:T(8,128)(2,1)} %hidden.1, bf16[1280,1024]{1,0:T(8,128)(2,1)} %weight.1, f32[1,128]{1,0:T(1,128)} %bitcast.11, ...), custom_call_target="tpu_custom_call" | custom-call | tf_op jit(solution)/shard_map/pallas_call | solution.py:432
  11.6 0.6 %copy.12 = bf16[3,8,1024]{2,1,0:T(8,128)(2,1)} copy(bf16[3,8,1024]{2,1,0:T(8,128)(2,1)S(1)} %shard_map.100) | data formatting | bytes 98304
